TPU v7x, 32 devices: a whole 2x2x4 slice. The times are simulated.
32 devices in a mesh: dp: 8 (over y, x, core), tensor: 4 (over z).
Axes of the slice: x: 2, y: 2, z: 4, core: 2. Of those that a mesh axis runs over, the one named last changes fastest.
Arguments:
- hidden: bfloat16 [8192, 768], P('dp'), may hold values from -6 to 6
- out_grad: bfloat16 [8192, 768], P('dp'), may hold values from -6 to 6
- w_query: bfloat16 [768, 768], P(None, 'tensor'), may hold values from -0.21875 to 0.21875
- w_key: bfloat16 [768, 768], P(None, 'tensor'), may hold values from -0.21875 to 0.21875
- w_value: bfloat16 [768, 768], P(None, 'tensor'), may hold values from -0.21875 to 0.21875
- w_out: bfloat16 [768, 768], P('tensor'), may hold values from -2.5 to 2.5
- w_in: bfloat16 [768, 3072], P(None, 'tensor'), may hold values from -0.21875 to 0.21875
- w_down: bfloat16 [3072, 768], P('tensor'), may hold values from -0.109375 to 0.109375
- bucket_table: bfloat16 [512, 768], replicated, may hold values from -6 to 6
- gain_one: float32 [768], replicated, may hold values from 0.5 to 1.5
- bias_one: float32 [768], replicated, may hold values from -2 to 2
- gain_two: float32 [768], replicated, may hold values from 0.5 to 1.5
- bias_two: float32 [768], replicated, may hold values from -2 to 2
- rel_buckets: int32 [1023], replicated, may hold values from 0 to 511
- group_counts: int32 [8, 3], P('dp'), may hold values from 0 to 8, as said below
- key_mask: int32 [8192], P('dp'), may hold values from 0 to 1, as said below
Outputs:
- output: bfloat16 [8192, 768], P('dp')
- grad_hidden: bfloat16 [8192, 768], P('dp')
- grad_query: float32 [768, 768], P(None, 'tensor')
- grad_key: float32 [768, 768], P(None, 'tensor')
- grad_value: float32 [768, 768], P(None, 'tensor')
- grad_out: float32 [768, 768], P('tensor')
- grad_in: float32 [768, 3072], P(None, 'tensor')
- grad_down: float32 [3072, 768], P('tensor')
- grad_table: float32 [512, 768], replicated
- grad_gain_one: float32 [768], replicated
- grad_bias_one: float32 [768], replicated
- grad_gain_two: float32 [768], replicated
- grad_bias_two: float32 [768], replicated
Inputs may be any that keep to these rules, and one draw needn't show every extreme that they name: `group_counts`: in each row c0 512 + c1 512 / 2 + c2 512 / 4 = 1024; some row holds only sequences of 128 tokens. `key_mask`: every token whose position in its dp index's buffer is a multiple of 128 is real.
All inputs are finite; a program needn't handle non-finite values.
Results may differ from a plain program's by a relative error of at most 0.02.
Values may be sent and summed in bfloat16 or wider, within the bound.
No kernel may reach another device: no remote copies, remote signals or barrier semaphores. Data moves between devices by JAX's collectives and lax.ppermute only.
A program may use at most 192 MiB of HBM per device.

v0:
```python
import math

import jax
import jax.numpy as jnp
from jax import lax
from jax.experimental import pallas as pl
from jax.experimental.pallas import tpu as pltpu
from jax.sharding import PartitionSpec as P

NORM_EPS = 1e-07
HEAD_DIM = 64
SEQMAX = 512
TILE = 128
WINDOW = SEQMAX + TILE
OFFSETS = 2 * SEQMAX
NEGATIVE = -1e30
F32 = jnp.float32
BF16 = jnp.bfloat16


def score_factor():
    return 1.0 / math.sqrt(3.0 * HEAD_DIM)


def mm(left, right):
    return jnp.dot(left, right, preferred_element_type=F32)


def mm_nt(left, right):
    return lax.dot_general(left, right, (((1,), (1,)), ((), ())), preferred_element_type=F32)


def mm_tn(left, right):
    return lax.dot_general(left, right, (((0,), (0,)), ((), ())), preferred_element_type=F32)


def starts_of(places, counts_ref):
    long_end = SEQMAX * counts_ref[0, 0]
    mid_end = long_end + SEQMAX // 2 * counts_ref[0, 1]
    in_long = places < long_end
    in_mid = places < mid_end
    anchor = jnp.where(in_long, 0, jnp.where(in_mid, long_end, mid_end))
    shift = jnp.where(in_long, 9, jnp.where(in_mid, 8, 7))
    return anchor + lax.shift_left(lax.shift_right_logical(places - anchor, shift), shift)


def tile_iotas():
    rows = lax.broadcasted_iota(jnp.int32, (TILE, TILE), 0)
    lanes = lax.broadcasted_iota(jnp.int32, (TILE, TILE), 1)
    return rows, lanes


def lane_tiles(wide):
    return [wide[:, c : c + TILE] for c in range(0, wide.shape[1], TILE)]


def skew(wide):
    rows, lanes = tile_iotas()
    keep = lanes <= rows
    turned = [pltpu.roll(part, 1, 1, stride=1, stride_axis=0) for part in lane_tiles(wide)]
    return jnp.concatenate(
        [jnp.where(keep, turned[c], turned[c + 1]) for c in range(len(turned) - 1)], axis=1
    )


def unskew(flipped):
    rows, lanes = tile_iotas()
    late = lanes > rows
    turned = [pltpu.roll(part, 1, 1, stride=1, stride_axis=0) for part in lane_tiles(flipped)]
    zero = jnp.zeros((TILE, TILE), F32)
    turned = [zero] + turned + [zero]
    return jnp.concatenate(
        [jnp.where(late, turned[c], turned[c + 1]) for c in range(len(turned) - 1)], axis=1
    )


def window_of(tile_at):
    low = SEQMAX - TILE - tile_at
    return slice(low, low + WINDOW)


def one_hot_columns(rel_ref, row, buckets):
    ids = lax.broadcasted_iota(jnp.int32, (buckets, OFFSETS), 0)
    return (ids == rel_ref[row : row + 1, :]).astype(BF16)


def split_low(wide):
    high = wide.astype(BF16)
    return high, (wide - high.astype(F32)).astype(BF16)


def forward_kernel(
    hidden_ref, wq_ref, wk_ref, wv_ref, table_ref, rel_ref, counts_ref, mask_ref,
    q_ref, k_ref, v_ref, weights_ref, context_ref, pk_back_ref, pq_back_ref,
    pk_ref, pq_ref, bias_ref, rel_score_ref,
):
    block = pl.program_id(0)
    buckets = table_ref.shape[0]
    heads = wq_ref.shape[1] // HEAD_DIM

    @pl.when(block == 0)
    def tables():
        table = table_ref[...]
        pos_key = lax.dot_general(
            wk_ref[...], table, (((0,), (1,)), ((), ())), preferred_element_type=F32
        ).astype(BF16)
        pos_query = lax.dot_general(
            wq_ref[...], table, (((0,), (1,)), ((), ())), preferred_element_type=F32
        ).astype(BF16)
        plain = one_hot_columns(rel_ref, 0, buckets)
        pk_ref[...] = mm(pos_key, plain).astype(BF16)
        pq_ref[...] = mm(pos_query, plain).astype(BF16)
        back = one_hot_columns(rel_ref, 1, buckets)
        pk_back_ref[...] = mm(pos_key, back).astype(BF16)
        pq_back_ref[...] = mm(pos_query, back).astype(BF16)

    first = block * SEQMAX
    column = starts_of(lax.broadcasted_iota(jnp.int32, (SEQMAX, 1), 0) + first, counts_ref)
    row = starts_of(lax.broadcasted_iota(jnp.int32, (1, SEQMAX), 1) + first, counts_ref)
    row = jnp.where(mask_ref[0] == 1, row, -1)
    bias_ref[...] = jnp.where(column == row, 0.0, NEGATIVE)

    hidden = hidden_ref[...]
    q_ref[...] = mm(hidden, wq_ref[...]).astype(BF16)
    k_ref[...] = mm(hidden, wk_ref[...]).astype(BF16)
    v_ref[...] = mm(hidden, wv_ref[...]).astype(BF16)
    for head in range(heads):
        part = slice(head * HEAD_DIM, (head + 1) * HEAD_DIM)
        queries = q_ref[:, part]
        keys = k_ref[:, part]
        values = v_ref[:, part]
        for at in range(0, SEQMAX, TILE):
            rel = mm(keys[at : at + TILE], pq_ref[part, window_of(at)])
            rel_score_ref[at : at + TILE, :] = skew(rel)
        for at in range(0, SEQMAX, TILE):
            rows = slice(at, at + TILE)
            raw = mm_nt(queries[rows], keys)
            raw = raw + skew(mm(queries[rows], pk_ref[part, window_of(at)]))
            raw = raw + rel_score_ref[:, rows].T
            scaled = raw * score_factor() + bias_ref[rows, :]
            top = jnp.max(scaled, axis=-1, keepdims=True)
            exponent = jnp.exp(scaled - top)
            total = jnp.sum(exponent, axis=-1, keepdims=True)
            weights = exponent * (1.0 / total)
            weights_ref[0, head, rows, :] = weights
            context_ref[rows, part] = mm(weights.astype(BF16), values).astype(BF16)


def forward_attention(hidden, w_query, w_key, w_value, table, rel_rows, counts, key_mask):
    tokens, width = hidden.shape
    local = w_query.shape[1]
    heads = local // HEAD_DIM
    buckets = table.shape[0]
    blocks = tokens // SEQMAX
    whole = lambda *shape: pl.BlockSpec(shape, lambda b: (0,) * len(shape))
    rows = lambda w: pl.BlockSpec((SEQMAX, w), lambda b: (b, 0))
    shape = jax.ShapeDtypeStruct
    return pl.pallas_call(
        forward_kernel,
        grid=(blocks,),
        in_specs=[
            rows(width),
            whole(width, local),
            whole(width, local),
            whole(width, local),
            whole(buckets, width),
            whole(2, OFFSETS),
            pl.BlockSpec(memory_space=pltpu.SMEM),
            pl.BlockSpec((1, 1, SEQMAX), lambda b: (b, 0, 0)),
        ],
        out_specs=[
            rows(local),
            rows(local),
            rows(local),
            pl.BlockSpec((1, heads, SEQMAX, SEQMAX), lambda b: (b, 0, 0, 0)),
            rows(local),
            whole(local, OFFSETS),
            whole(local, OFFSETS),
        ],
        out_shape=[
            shape((tokens, local), BF16),
            shape((tokens, local), BF16),
            shape((tokens, local), BF16),
            shape((blocks, heads, SEQMAX, SEQMAX), F32),
            shape((tokens, local), BF16),
            shape((local, OFFSETS), BF16),
            shape((local, OFFSETS), BF16),
        ],
        scratch_shapes=[
            pltpu.VMEM((local, OFFSETS), BF16),
            pltpu.VMEM((local, OFFSETS), BF16),
            pltpu.VMEM((SEQMAX, SEQMAX), F32),
            pltpu.VMEM((SEQMAX, SEQMAX), F32),
        ],
        compiler_params=pltpu.CompilerParams(
            dimension_semantics=("arbitrary",), vmem_limit_bytes=40 * 2**20
        ),
        cost_estimate=pl.CostEstimate(
            flops=8_000_000_000, bytes_accessed=12_000_000, transcendentals=1_600_000
        ),
        name="attention_forward",
    )(hidden, w_query, w_key, w_value, table, rel_rows, counts, key_mask.reshape(blocks, 1, SEQMAX))


def backward_kernel(
    cg_ref, q_ref, k_ref, v_ref, weights_ref, pk_back_ref, pq_back_ref,
    hidden_ref, wq_ref, wk_ref, wv_ref, table_ref, rel_ref,
    part_ref, grads_ref, pos_ref,
    ds_ref, rows_ref, rg_key_ref, rg_query_ref, sum_ref,
):
    block = pl.program_id(0)
    blocks = pl.num_programs(0)
    local = wq_ref.shape[1]
    heads = local // HEAD_DIM
    buckets = table_ref.shape[0]

    @pl.when(block == 0)
    def clear():
        rg_key_ref[...] = jnp.zeros_like(rg_key_ref)
        rg_query_ref[...] = jnp.zeros_like(rg_query_ref)
        sum_ref[...] = jnp.zeros_like(sum_ref)

    tile_rows, tile_lanes = tile_iotas()
    flip = (tile_rows + tile_lanes == TILE - 1).astype(BF16)

    def flipped(low):
        return jnp.concatenate([mm(part, flip) for part in lane_tiles(low)], axis=1)

    for head in range(heads):
        part = slice(head * HEAD_DIM, (head + 1) * HEAD_DIM)
        at_k = slice(local + head * HEAD_DIM, local + (head + 1) * HEAD_DIM)
        at_v = slice(2 * local + head * HEAD_DIM, 2 * local + (head + 1) * HEAD_DIM)
        queries = q_ref[:, part]
        keys = k_ref[:, part]
        values = v_ref[:, part]
        cotangent = cg_ref[:, part]
        value_grad = jnp.zeros((SEQMAX, HEAD_DIM), F32)
        for at in range(0, SEQMAX, TILE):
            rows = slice(at, at + TILE)
            weights = weights_ref[0, head, rows, :]
            weight_grad = mm_nt(cotangent[rows], values)
            inner = jnp.sum(weights * weight_grad, axis=-1, keepdims=True)
            score_grad = (weights * (weight_grad - inner) * score_factor()).astype(BF16)
            ds_ref[rows, :] = score_grad
            value_grad = value_grad + mm_tn(weights.astype(BF16), cotangent[rows])
            by_offset = unskew(flipped(score_grad)).astype(BF16)
            window = window_of(at)
            query_grad = mm(score_grad, keys) + mm_nt(by_offset, pk_back_ref[part, window])
            rows_ref[rows, part] = query_grad.astype(BF16)
            rg_key_ref[part, window] += mm_tn(queries[rows], by_offset)
        rows_ref[:, at_v] = value_grad.astype(BF16)
        for at in range(0, SEQMAX, TILE):
            rows = slice(at, at + TILE)
            turned = ds_ref[:, rows].T
            by_offset = unskew(flipped(turned)).astype(BF16)
            window = window_of(at)
            key_grad = mm(turned, queries) + mm_nt(by_offset, pq_back_ref[part, window])
            rows_ref[rows, at_k] = key_grad.astype(BF16)
            rg_query_ref[part, window] += mm_tn(keys[rows], by_offset)
    total = mm_nt(rows_ref[:, :local], wq_ref[...])
    total = total + mm_nt(rows_ref[:, local : 2 * local], wk_ref[...])
    total = total + mm_nt(rows_ref[:, 2 * local :], wv_ref[...])
    part_ref[...] = total.astype(BF16)
    sum_ref[...] += mm_tn(hidden_ref[...], rows_ref[...])

    @pl.when(block == blocks - 1)
    def finish():
        back = one_hot_columns(rel_ref, 1, buckets)

        def by_bucket(rg_ref):
            high, low = split_low(rg_ref[...])
            return (mm_nt(high, back) + mm_nt(low, back)).T

        def through_table(grad):
            high, low = split_low(grad)
            return mm_tn(table_ref[...], high) + mm_tn(table_ref[...], low)

        pos_key = by_bucket(rg_key_ref)
        pos_query = by_bucket(rg_query_ref)
        pos_ref[:, :local] = pos_key.astype(pos_ref.dtype)
        pos_ref[:, local:] = pos_query.astype(pos_ref.dtype)
        grads_ref[:, :local] = (sum_ref[:, :local] + through_table(pos_query)).astype(
            grads_ref.dtype
        )
        grads_ref[:, local : 2 * local] = (
            sum_ref[:, local : 2 * local] + through_table(pos_key)
        ).astype(grads_ref.dtype)
        grads_ref[:, 2 * local :] = sum_ref[:, 2 * local :].astype(grads_ref.dtype)


def backward_attention(
    context_grad, queries, keys, values, weights, pk_back, pq_back,
    hidden, w_query, w_key, w_value, table, rel_rows, kind,
):
    tokens, width = hidden.shape
    local = w_query.shape[1]
    heads = local // HEAD_DIM
    buckets = table.shape[0]
    blocks = tokens // SEQMAX
    whole = lambda *shape: pl.BlockSpec(shape, lambda b: (0,) * len(shape))
    rows = lambda w: pl.BlockSpec((SEQMAX, w), lambda b: (b, 0))
    shape = jax.ShapeDtypeStruct
    return pl.pallas_call(
        backward_kernel,
        grid=(blocks,),
        in_specs=[
            rows(local),
            rows(local),
            rows(local),
            rows(local),
            pl.BlockSpec((1, heads, SEQMAX, SEQMAX), lambda b: (b, 0, 0, 0)),
            whole(local, OFFSETS),
            whole(local, OFFSETS),
            rows(width),
            whole(width, local),
            whole(width, local),
            whole(width, local),
            whole(buckets, width),
            whole(2, OFFSETS),
        ],
        out_specs=[rows(width), whole(width, 3 * local), whole(buckets, 2 * local)],
        out_shape=[
            shape((tokens, width), BF16),
            shape((width, 3 * local), kind),
            shape((buckets, 2 * local), kind),
        ],
        scratch_shapes=[
            pltpu.VMEM((SEQMAX, SEQMAX), BF16),
            pltpu.VMEM((SEQMAX, 3 * local), BF16),
            pltpu.VMEM((local, OFFSETS), F32),
            pltpu.VMEM((local, OFFSETS), F32),
            pltpu.VMEM((width, 3 * local), F32),
        ],
        compiler_params=pltpu.CompilerParams(
            dimension_semantics=("arbitrary",), vmem_limit_bytes=48 * 2**20
        ),
        cost_estimate=pl.CostEstimate(
            flops=16_000_000_000, bytes_accessed=16_000_000, transcendentals=0
        ),
        name="attention_backward",
    )(
        context_grad, queries, keys, values, weights, pk_back, pq_back,
        hidden, w_query, w_key, w_value, table, rel_rows,
    )


def offset_rows(rel_buckets):
    plain = jnp.concatenate([rel_buckets[::-1], rel_buckets[:1]])
    back = plain.reshape(OFFSETS // TILE, TILE)[:, ::-1].reshape(OFFSETS)
    return jnp.stack([plain, back])


def exact_dot(left, right):
    return jnp.dot(left, right, precision=lax.Precision.HIGHEST, preferred_element_type=F32)


def float_dot(left, right):
    return jnp.dot(left, right, preferred_element_type=F32)


def layer_norm(resid, gain, offset):
    average = jnp.mean(resid, axis=-1, keepdims=True)
    centered = resid - average
    variance = jnp.mean(centered * centered, axis=-1, keepdims=True)
    return centered * lax.rsqrt(variance + NORM_EPS) * gain + offset


def exact_gelu(pre_act):
    return jax.nn.gelu(pre_act, approximate=False)


def shards(
    hidden,
    out_grad,
    w_query,
    w_key,
    w_value,
    w_out,
    w_in,
    w_down,
    bucket_table,
    gain_one,
    bias_one,
    gain_two,
    bias_two,
    rel_buckets,
    group_counts,
    key_mask,
):
    local_width = w_query.shape[1]
    rel_rows = offset_rows(rel_buckets)
    query_rows, key_rows, value_rows, weights, context, pk_back, pq_back = forward_attention(
        hidden, w_query, w_key, w_value, bucket_table, rel_rows, group_counts, key_mask
    )
    attn_out = lax.psum(float_dot(context, w_out).astype(jnp.bfloat16), "tensor").astype(
        jnp.float32
    )
    first_norm, norm_one_back = jax.vjp(
        layer_norm, hidden.astype(jnp.float32) + attn_out, gain_one, bias_one
    )
    first_low = first_norm.astype(jnp.bfloat16)
    pre_act = float_dot(first_low, w_in)
    activated_full, gelu_back = jax.vjp(exact_gelu, pre_act)
    activated = activated_full.astype(jnp.bfloat16)
    ffn_out = lax.psum(float_dot(activated, w_down).astype(jnp.bfloat16), "tensor").astype(
        jnp.float32
    )
    second_norm, norm_two_back = jax.vjp(layer_norm, first_norm + ffn_out, gain_two, bias_two)
    output = second_norm.astype(jnp.bfloat16)
    second_grad, grad_gain_two, grad_bias_two = norm_two_back(out_grad.astype(jnp.float32))
    ffn_grad = second_grad.astype(jnp.bfloat16)
    down_local = jnp.einsum("tf,td->fd", activated, ffn_grad, preferred_element_type=jnp.float32)
    act_grad = jnp.einsum("td,fd->tf", ffn_grad, w_down, preferred_element_type=jnp.float32)
    pre_grad = gelu_back(act_grad)[0].astype(jnp.bfloat16)
    in_local = jnp.einsum("tc,tf->cf", first_low, pre_grad, preferred_element_type=jnp.float32)
    back_part = jnp.einsum("tf,cf->tc", pre_grad, w_in, preferred_element_type=jnp.float32)
    first_grad = second_grad + lax.psum(back_part.astype(jnp.bfloat16), "tensor").astype(
        jnp.float32
    )
    resid_grad, grad_gain_one, grad_bias_one = norm_one_back(first_grad)
    attn_grad = resid_grad.astype(jnp.bfloat16)
    out_local = jnp.einsum("tk,td->kd", context, attn_grad, preferred_element_type=jnp.float32)
    context_grad = jnp.einsum(
        "td,kd->tk", attn_grad, w_out, preferred_element_type=jnp.float32
    ).astype(jnp.bfloat16)

    hidden_part, local_grads, pos_grads = backward_attention(
        context_grad, query_rows, key_rows, value_rows, weights, pk_back, pq_back,
        hidden, w_query, w_key, w_value, bucket_table, rel_rows, F32,
    )
    grad_hidden = (
        resid_grad + lax.psum(hidden_part.astype(jnp.bfloat16), "tensor").astype(jnp.float32)
    ).astype(jnp.bfloat16)
    query_local = local_grads[:, :local_width]
    key_local = local_grads[:, local_width : 2 * local_width]
    value_local = local_grads[:, 2 * local_width :]
    key_wide = w_key.astype(jnp.float32)
    query_wide = w_query.astype(jnp.float32)
    table_part = exact_dot(pos_grads[:, :local_width], key_wide.T)
    table_part = table_part + exact_dot(pos_grads[:, local_width:], query_wide.T)
    shares = (
        lax.psum_scatter(query_local, "dp", scatter_dimension=0, tiled=True),
        lax.psum_scatter(key_local, "dp", scatter_dimension=0, tiled=True),
        lax.psum_scatter(value_local, "dp", scatter_dimension=0, tiled=True),
        lax.psum_scatter(out_local, "dp", scatter_dimension=1, tiled=True),
        lax.psum_scatter(in_local, "dp", scatter_dimension=0, tiled=True),
        lax.psum_scatter(down_local, "dp", scatter_dimension=1, tiled=True),
        lax.psum_scatter(grad_gain_one, "dp", scatter_dimension=0, tiled=True),
        lax.psum_scatter(grad_bias_one, "dp", scatter_dimension=0, tiled=True),
        lax.psum_scatter(grad_gain_two, "dp", scatter_dimension=0, tiled=True),
        lax.psum_scatter(grad_bias_two, "dp", scatter_dimension=0, tiled=True),
    )
    gathered = (
        lax.all_gather(shares[0].astype(jnp.bfloat16), "dp", axis=0, tiled=True).astype(
            jnp.float32
        ),
        lax.all_gather(shares[1].astype(jnp.bfloat16), "dp", axis=0, tiled=True).astype(
            jnp.float32
        ),
        lax.all_gather(shares[2].astype(jnp.bfloat16), "dp", axis=0, tiled=True).astype(
            jnp.float32
        ),
        lax.all_gather(shares[3].astype(jnp.bfloat16), "dp", axis=1, tiled=True).astype(
            jnp.float32
        ),
        lax.all_gather(shares[4].astype(jnp.bfloat16), "dp", axis=0, tiled=True).astype(
            jnp.float32
        ),
        lax.all_gather(shares[5].astype(jnp.bfloat16), "dp", axis=1, tiled=True).astype(
            jnp.float32
        ),
        lax.all_gather(shares[6].astype(jnp.bfloat16), "dp", axis=0, tiled=True).astype(
            jnp.float32
        ),
        lax.all_gather(shares[7].astype(jnp.bfloat16), "dp", axis=0, tiled=True).astype(
            jnp.float32
        ),
        lax.all_gather(shares[8].astype(jnp.bfloat16), "dp", axis=0, tiled=True).astype(
            jnp.float32
        ),
        lax.all_gather(shares[9].astype(jnp.bfloat16), "dp", axis=0, tiled=True).astype(
            jnp.float32
        ),
    )
    grad_query = gathered[0]
    grad_key = gathered[1]
    table_share = lax.psum_scatter(table_part, ("dp", "tensor"), scatter_dimension=0, tiled=True)
    grad_table = lax.all_gather(table_share, ("dp", "tensor"), axis=0, tiled=True)
    return (
        output,
        grad_hidden,
        grad_query,
        grad_key,
        gathered[2],
        gathered[3],
        gathered[4],
        gathered[5],
        grad_table,
        gathered[6],
        gathered[7],
        gathered[8],
        gathered[9],
    )


def solution(mesh):
    in_specs = (
        P("dp", None),
        P("dp", None),
        P(None, "tensor"),
        P(None, "tensor"),
        P(None, "tensor"),
        P("tensor", None),
        P(None, "tensor"),
        P("tensor", None),
        P(),
        P(),
        P(),
        P(),
        P(),
        P(),
        P("dp", None),
        P("dp"),
    )
    out_specs = (
        P("dp", None),
        P("dp", None),
        P(None, "tensor"),
        P(None, "tensor"),
        P(None, "tensor"),
        P("tensor", None),
        P(None, "tensor"),
        P("tensor", None),
        P(),
        P(),
        P(),
        P(),
        P(),
    )
    return jax.shard_map(shards, mesh=mesh, in_specs=in_specs, out_specs=out_specs, check_vma=False)
```

profile of v0, /device:TPU:31, one launch (start us, length us, event | category | flops | bytes accessed | tf_op | source)
XLA Modules:
  0.0 821.4 jit_solution(7873302622290110338)
XLA Ops:
  18.5 18.9 %attention_forward.1 = (bf16[1024,192]{1,0:T(8,128)(2,1)S(1)}, bf16[1024,192]{1,0:T(8,128)(2,1)S(1)}, bf16[1024,192]{1,0:T(8,128)(2,1)S(1)}, f32[2,3,512,512]{3,...) custom-call(bf16[1024,768]{1,0:T(8,128)(2,1)S(1)} %copy-done.2, ...), custom_call_target="tpu_custom_call" | custom-call | flops 8000000000 | bytes 12000000 | tf_op jit(solution)/shard_map/attention_forward/pallas_call | solution.py:158
  46.8 68.2 %all-reduce.15.cloned.1.call-done = bf16[1024,768]{1,0:T(8,128)(2,1)} async-done(((bf16[1024,768]{1,0:T(8,128)(2,1)}), bf16[1024,768]{1,0:T(8,128)(2,1)}) %all-reduce.15.cloned.1.call-update) | async-done | bytes 1572880 | tf_op jit(solution)/shard_map/psum | solution.py:395
  117.8 9.7 %multiply_convert_fusion = (bf16[1024,768]{1,0:T(8,128)(2,1)S(1)}, f32[1024,768]{1,0:T(8,128)}, f32[1024,768]{1,0:T(8,128)}) fusion(bf16[768,768]{1,0:T(8,128)(2,1)S(1)} %copy-done, f32[768]{0:T(1024)S(1)} %copy-done.38, f32[768]{0:T(1024)S(1)} %copy-done.36, f32[1024]{0:T(1024)S(1)} %fusion.16, f32[1024]{0:T(1024)S(1)} %broadcast_multiply_fusion.1, ...), kind=kOutput, calls=%fused_computation.19 | convolution fusion | flops 1265369088 | bytes 12204032 | tf_op jit(solution)/shard_map/dot_general | solution.py:358
  131.3 68.3 %all-reduce.17.cloned.1.call-done = bf16[1024,768]{1,0:T(8,128)(2,1)} async-done(((bf16[1024,768]{1,0:T(8,128)(2,1)}), bf16[1024,768]{1,0:T(8,128)(2,1)}) %all-reduce.17.cloned.1.call-update) | async-done | bytes 1572880 | tf_op jit(solution)/shard_map/psum | solution.py:405
  199.5 3.1 fusion.29
  215.7 12.7 %reduce-scatter.18.cloned.1.call-start = ((), (), s32[]{:S(2)}) async-start(), calls=%async_computation.16 | async-start | bytes 2654208 | tf_op jit(solution)/shard_map/reduce_scatter | solution.py:447
  228.3 5.3 fusion.18
  233.8 5.2 fusion.20
  239.0 45.0 %all-reduce.19.cloned.1.call-done = bf16[1024,768]{1,0:T(8,128)(2,1)} async-done(((bf16[1024,768]{1,0:T(8,128)(2,1)}), bf16[1024,768]{1,0:T(8,128)(2,1)}) %all-reduce.19.cloned.1.call-update) | async-done | bytes 1572880 | tf_op jit(solution)/shard_map/psum | solution.py:417
  284.0 4.0 multiply_reduce_fusion
  298.7 32.7 %attention_backward.1 = (bf16[1024,768]{1,0:T(8,128)(2,1)}, f32[768,576]{1,0:T(8,128)}, f32[512,384]{1,0:T(8,128)S(1)}) custom-call(bf16[1024,192]{1,0:T(8,128)(2,1)S(1)} %copy.56.cg_ref, bf16[1024,192]{1,0:T(8,128)(2,1)S(1)} %copy-done.16, bf16[1024,192]{1,0:T(8,128)(2,1)S(1)} %copy-done.18, bf16[1024,192]{1,0:T(8,128)(2,1)S(1)} %copy-done.20, ...), custom_call_target="tpu_custom_call" | custom-call | flops 16000000000 | bytes 16000000 | tf_op jit(solution)/shard_map/attention_backward/pallas_call | solution.py:303
  334.3 3.7 convolution_bitcast_fusion
  338.1 3.5 fusion.31
  345.5 31.3 %reduce-scatter.16.cloned.1.call-done = f32[96,768]{1,0:T(8,128)} async-done(((f32[768,768]{1,0:T(8,128)}), f32[96,768]{1,0:T(8,128)}) %reduce-scatter.16.cloned.1.call-update) | async-done | bytes 294928 | tf_op jit(solution)/shard_map/reduce_scatter | solution.py:446
  378.5 98.7 %reduce-scatter.20.cloned.1.call-done = f32[16,768]{1,0:T(8,128)} async-done(((f32[512,768]{1,0:T(8,128)}), f32[16,768]{1,0:T(8,128)}) %reduce-scatter.20.cloned.1.call-update) | async-done | bytes 49168 | tf_op jit(solution)/shard_map/reduce_scatter | solution.py:487
  479.1 22.3 %all-reduce.8 = (bf16[768]{0:T(1024)(128)(2,1)S(1)}, bf16[768]{0:T(1024)(128)(2,1)S(1)}, bf16[768]{0:T(1024)(128)(2,1)S(1)}, bf16[768]{0:T(1024)(128)(2,1)S(1)}) all-reduce(f32[768]{0:T(1024)S(1)} %get-tuple-element.72, f32[768]{0:T(1024)S(1)} %get-tuple-element.76, ...), channel_id=9, replica_groups=mesh['dp'=8,'tensor'=4] {'dp'}, use_global_device_ids=true, to_apply=%region_20.0.clone | all-reduce | flops 3072 | bytes 18432
  502.4 12.0 %all-reduce.9 = (bf16[768]{0:T(1024)(128)(2,1)S(1)}, bf16[768]{0:T(1024)(128)(2,1)S(1)}, bf16[768]{0:T(1024)(128)(2,1)S(1)}, bf16[768]{0:T(1024)(128)(2,1)S(1)}) all-reduce(bf16[768]{0:T(1024)(128)(2,1)S(1)} %dynamic-update-slice, bf16[768]{0:T(1024)(128)(2,1)S(1)} %dynamic-update-slice.1, ...), channel_id=1, replica_groups=mesh['dp'=8,'tensor'=4] {'dp'}, use_global_device_ids=true, to_apply=%add | all-reduce | flops 3072 | bytes 12288
  517.9 11.6 %all_gather.36 = bf16[192,768]{0,1:T(8,128)(2,1)S(1)} all-gather(bf16[192,96]{0,1:T(8,128)(2,1)S(1)} %copy.60), channel_id=1, replica_groups=mesh['dp'=8,'tensor'=4] {'dp'}, dimensions={1}, use_global_device_ids=true | all-gather | bytes 331776 | tf_op jit(solution)/shard_map/all_gather | solution.py:463
  530.5 24.2 %reduce-scatter.10.cloned.1.call-done = f32[96,192]{1,0:T(8,128)} async-done(((f32[768,192]{1,0:T(8,128)}), f32[96,192]{1,0:T(8,128)}) %reduce-scatter.10.cloned.1.call-update) | async-done | bytes 73744 | tf_op jit(solution)/shard_map/reduce_scatter | solution.py:442
  555.6 10.3 %all_gather.33 = bf16[768,192]{1,0:T(8,128)(2,1)S(1)} all-gather(bf16[96,192]{1,0:T(8,128)(2,1)S(1)} %convert_element_type.130), channel_id=1, replica_groups=mesh['dp'=8,'tensor'=4] {'dp'}, dimensions={0}, use_global_device_ids=true | all-gather | bytes 331776 | tf_op jit(solution)/shard_map/all_gather | solution.py:454
  566.8 26.0 %reduce-scatter.12.cloned.1.call-done = f32[96,192]{1,0:T(8,128)} async-done(((f32[768,192]{1,0:T(8,128)}), f32[96,192]{1,0:T(8,128)}) %reduce-scatter.12.cloned.1.call-update) | async-done | bytes 73744 | tf_op jit(solution)/shard_map/reduce_scatter | solution.py:443
  593.7 10.3 %all_gather.34 = bf16[768,192]{1,0:T(8,128)(2,1)S(1)} all-gather(bf16[96,192]{1,0:T(8,128)(2,1)S(1)} %convert_element_type.132), channel_id=1, replica_groups=mesh['dp'=8,'tensor'=4] {'dp'}, dimensions={0}, use_global_device_ids=true | all-gather | bytes 331776 | tf_op jit(solution)/shard_map/all_gather | solution.py:457
  605.0 25.8 %reduce-scatter.14.cloned.1.call-done = f32[96,192]{1,0:T(8,128)} async-done(((f32[768,192]{1,0:T(8,128)}), f32[96,192]{1,0:T(8,128)}) %reduce-scatter.14.cloned.1.call-update) | async-done | bytes 73744 | tf_op jit(solution)/shard_map/reduce_scatter | solution.py:444
  631.8 10.3 %all_gather.35 = bf16[768,192]{1,0:T(8,128)(2,1)S(1)} all-gather(bf16[96,192]{1,0:T(8,128)(2,1)S(1)} %convert_element_type.134), channel_id=1, replica_groups=mesh['dp'=8,'tensor'=4] {'dp'}, dimensions={0}, use_global_device_ids=true | all-gather | bytes 331776 | tf_op jit(solution)/shard_map/all_gather | solution.py:460
  643.1 59.4 %all-reduce.21.cloned.1.call-done = bf16[1024,768]{1,0:T(8,128)(2,1)} async-done(((bf16[1024,768]{1,0:T(8,128)(2,1)}), bf16[1024,768]{1,0:T(8,128)(2,1)}) %all-reduce.21.cloned.1.call-update) | async-done | bytes 1572880 | tf_op jit(solution)/shard_map/psum | solution.py:432
  702.5 3.9 add_convert_fusion
  706.4 22.2 %all-gather.6.cloned.1.call-done = bf16[768,768]{0,1:T(8,128)(2,1)} async-done(((bf16[768,96]{0,1:T(8,128)(2,1)}), bf16[768,768]{0,1:T(8,128)(2,1)}) %all-gather.6.cloned.1.call-update) | async-done | bytes 1179664 | tf_op jit(solution)/shard_map/all_gather | solution.py:469
  728.6 2.8 copy.65
  731.4 23.7 %all-gather.4.cloned.1.call-done = bf16[768,768]{1,0:T(8,128)(2,1)} async-done(((bf16[96,768]{1,0:T(8,128)(2,1)}), bf16[768,768]{1,0:T(8,128)(2,1)}) %all-gather.4.cloned.1.call-update) | async-done | bytes 1179664 | tf_op jit(solution)/shard_map/all_gather | solution.py:466
  755.1 2.8 convert_element_type.139
  758.0 53.8 %all-gather.8.cloned.1.call-done = f32[512,768]{1,0:T(8,128)} async-done(((f32[16,768]{1,0:T(8,128)}), f32[512,768]{1,0:T(8,128)}) %all-gather.8.cloned.1.call-update) | async-done | bytes 1572880 | tf_op jit(solution)/shard_map/all_gather | solution.py:488
  811.8 2.7 copy.77
  (183 shorter events, 70.8 us)
Async XLA Ops:
  7.2 110.6 %copy-start = (bf16[768,768]{1,0:T(8,128)(2,1)S(1)}, bf16[768,768]{1,0:T(8,128)(2,1)}, u32[]{:S(2)}) copy-start(bf16[768,768]{1,0:T(8,128)(2,1)} %param.22) | copy-start | bytes 3538948
  7.2 107.7 %all-reduce.15.cloned.1.call-start = ((), (), s32[]{:S(2)}) async-start(), calls=%async_computation.7 | async-start | bytes 3145728 | tf_op jit(solution)/shard_map/psum | solution.py:395
  18.5 26.2 %copy-start.32 = (bf16[192,768]{1,0:T(8,128)(2,1)S(1)}, bf16[192,768]{1,0:T(8,128)(2,1)}, u32[]{:S(2)}) copy-start(bf16[192,768]{1,0:T(8,128)(2,1)} %param.21) | copy-start | bytes 884740
  44.7 70.2 %copy-start.3 = (bf16[1024,768]{1,0:T(8,128)(2,1)S(1)}, bf16[1024,768]{1,0:T(8,128)(2,1)}, u32[]{:S(2)}) copy-start(bf16[1024,768]{1,0:T(8,128)(2,1)} %hidden_ref.3) | copy-start | bytes 4718596
  46.5 71.3 %copy-start.36 = (f32[768]{0:T(1024)S(1)}, f32[768]{0:T(1024)}, u32[]{:S(2)}) copy-start(f32[768]{0:T(1024)} %param.25) | copy-start | bytes 9220
  46.5 71.3 %copy-start.38 = (f32[768]{0:T(1024)S(1)}, f32[768]{0:T(1024)}, u32[]{:S(2)}) copy-start(f32[768]{0:T(1024)} %param.26) | copy-start | bytes 9220
  46.5 153.1 %all-reduce.17.cloned.1.call-start = ((), (), s32[]{:S(2)}) async-start(), calls=%async_computation.8 | async-start | bytes 3145728 | tf_op jit(solution)/shard_map/psum | solution.py:405
  117.8 10.9 %copy-start.41 = (bf16[768,768]{1,0:T(8,128)(2,1)S(1)}, bf16[768,768]{1,0:T(8,128)(2,1)}, u32[]{:S(2)}) copy-start(bf16[768,768]{1,0:T(8,128)(2,1)} %param.23) | copy-start | bytes 3538948
  131.2 152.7 %all-reduce.19.cloned.1.call-start = ((), (), s32[]{:S(2)}) async-start(), calls=%async_computation.9 | async-start | bytes 3145728 | tf_op jit(solution)/shard_map/psum | solution.py:417
  205.4 4.1 copy-start.44
  208.0 4.0 copy-start.28
  215.7 128.1 %reduce-scatter.18.cloned.1.call-start = ((), (), s32[]{:S(2)}) async-start(), calls=%async_computation.16 | async-start | bytes 2654208 | tf_op jit(solution)/shard_map/reduce_scatter | solution.py:447
  233.7 143.1 %reduce-scatter.16.cloned.1.call-start = ((), (), s32[]{:S(2)}) async-start(), calls=%async_computation.14 | async-start | bytes 2654208 | tf_op jit(solution)/shard_map/reduce_scatter | solution.py:446
  238.9 238.2 %reduce-scatter.20.cloned.1.call-start = ((), (), s32[]{:S(2)}) async-start(), calls=%async_computation.18 | async-start | bytes 1622016 | tf_op jit(solution)/shard_map/reduce_scatter | solution.py:487
  284.0 4.1 copy-start.27
  284.0 4.2 copy-start.29
  284.0 4.7 copy-start.30
  288.7 3.7 copy-start.33
  290.7 2.7 copy-start.5
  290.7 2.7 copy-start.7
  298.7 32.7 %copy-start.34 = (bf16[768,192]{0,1:T(8,128)(2,1)S(1)}, bf16[768,192]{0,1:T(8,128)(2,1)}, u32[]{:S(2)}) copy-start(bf16[768,192]{0,1:T(8,128)(2,1)} %param.19) | copy-start | bytes 884740
  298.7 33.5 %copy-start.35 = (bf16[768,192]{0,1:T(8,128)(2,1)S(1)}, bf16[768,192]{0,1:T(8,128)(2,1)}, u32[]{:S(2)}) copy-start(bf16[768,192]{0,1:T(8,128)(2,1)} %param.18) | copy-start | bytes 884740
  334.2 182.6 %reduce-scatter.22.cloned.1.call-start = ((), (), s32[]{:S(2)}) async-start(), calls=%async_computation.20 | async-start | bytes 884736
  338.0 216.6 %reduce-scatter.10.cloned.1.call-start = ((), (), s32[]{:S(2)}) async-start(), calls=%async_computation.11 | async-start | bytes 884736 | tf_op jit(solution)/shard_map/reduce_scatter | solution.py:442
  341.6 135.6 %copy-start.40 = (u32[32]{0:T(128)S(1)}, u32[32]{0:T(128)}, u32[]{:S(2)}) copy-start(u32[32]{0:T(128)} %constant.80) | copy-start | bytes 388
  341.6 251.2 %reduce-scatter.12.cloned.1.call-start = ((), (), s32[]{:S(2)}) async-start(), calls=%async_computation.12 | async-start | bytes 884736 | tf_op jit(solution)/shard_map/reduce_scatter | solution.py:443
  342.3 288.5 %reduce-scatter.14.cloned.1.call-start = ((), (), s32[]{:S(2)}) async-start(), calls=%async_computation.13 | async-start | bytes 884736 | tf_op jit(solution)/shard_map/reduce_scatter | solution.py:444
  342.9 359.5 %all-reduce.21.cloned.1.call-start = ((), (), s32[]{:S(2)}) async-start(), calls=%async_computation.10 | async-start | bytes 3145728 | tf_op jit(solution)/shard_map/psum | solution.py:432
  343.7 384.9 %all-gather.6.cloned.1.call-start = ((), (), s32[]{:S(2)}) async-start(), calls=%async_computation.17 | async-start | bytes 1327104 | tf_op jit(solution)/shard_map/all_gather | solution.py:469
  345.4 409.7 %all-gather.4.cloned.1.call-start = ((), (), s32[]{:S(2)}) async-start(), calls=%async_computation.15 | async-start | bytes 1327104 | tf_op jit(solution)/shard_map/all_gather | solution.py:466
  378.4 433.4 %all-gather.8.cloned.1.call-start = ((), (), s32[]{:S(2)}) async-start(), calls=%async_computation.19 | async-start | bytes 1622016 | tf_op jit(solution)/shard_map/all_gather | solution.py:488
  728.6 85.9 %copy-start.1 = (bf16[768,768]{1,0:T(8,128)(2,1)S(1)}, bf16[768,768]{1,0:T(8,128)(2,1)}, u32[]{:S(2)}) copy-start(bf16[768,768]{1,0:T(8,128)(2,1)} %param.22) | copy-start | bytes 3538948
  (29 other events, 42.0 us)
Sparse Core Ops, SparseCore 0:
  46.6 68.3 all-reduce.14
  131.4 68.1 all-reduce.16
  215.8 68.1 all-reduce.18
  287.8 42.3 reduce-scatter.17
  334.3 42.4 reduce-scatter.15
  382.4 94.6 reduce-scatter.19
  480.3 36.0 reduce-scatter.21
  519.6 35.0 reduce-scatter.9
  557.8 34.9 reduce-scatter.11
  595.8 34.9 reduce-scatter.13
  633.8 68.6 all-reduce.20
  704.2 24.3 all-gather.5
  731.0 24.0 all-gather.3
  757.9 53.9 all-gather.7
where the time goes:
time: 833 us; the launch traced here: 821 us
  waiting for transfers between devices  549 us (66%)
  blocking collectives  76.8 us (9%)
  Pallas kernels  51.6 us (6%)
  local copies, waits for them, and re-layouts  45.2 us (5%)
  matrix products  36.7 us (4%)
  other arithmetic  32.9 us (4%)
  between operations  16.1 us (2%)
  starting transfers between devices  13.5 us (2%)
    reduce_scatter x1, waiting for transfers between devices, shards(): lax.psum_scatter(table_part, ('dp', 'tensor'), scatter_dimension=0, tiled...  98.7 us
    psum x1, waiting for transfers between devices, shards(): lax.psum(float_dot(activated, w_down).astype(jnp.bfloat16), 'tensor')  68.3 us
    psum x1, waiting for transfers between devices, shards(): lax.psum(float_dot(context, w_out).astype(jnp.bfloat16), 'tensor')  68.2 us
    psum x1, waiting for transfers between devices, shards(): lax.psum(hidden_part.astype(jnp.bfloat16), 'tensor').astype(jnp.float32)  59.4 us
    all_gather x1, waiting for transfers between devices, shards(): lax.all_gather(table_share, ('dp', 'tensor'), axis=0, tiled=True)  53.8 us
    psum x1, waiting for transfers between devices, shards(): lax.psum(back_part.astype(jnp.bfloat16), 'tensor').astype(jnp.float32)  45 us
    unnamed x119, local copies, waits for them, and re-layouts  40 us
    unnamed x2, blocking collectives  34.3 us
  transfers between devices with their start and end apart: 14, of which 12 were waited for; matrix products, arithmetic and copies ran while one was open for 6% of the time, Pallas kernels for 4%

commit v1 on v0

--- a/solution.py
+++ b/solution.py
@@ -1,3 +1,4 @@
+import functools
 import math
 
 import jax
@@ -203,7 +204,7 @@
 
 
 def backward_kernel(
-    cg_ref, q_ref, k_ref, v_ref, weights_ref, pk_back_ref, pq_back_ref,
+    order_ref, cg_ref, q_ref, k_ref, v_ref, weights_ref, pk_back_ref, pq_back_ref,
     hidden_ref, wq_ref, wk_ref, wv_ref, table_ref, rel_ref,
     part_ref, grads_ref, pos_ref,
     ds_ref, rows_ref, rg_key_ref, rg_query_ref, sum_ref,
@@ -233,16 +234,16 @@
         queries = q_ref[:, part]
         keys = k_ref[:, part]
         values = v_ref[:, part]
-        cotangent = cg_ref[:, part]
         value_grad = jnp.zeros((SEQMAX, HEAD_DIM), F32)
         for at in range(0, SEQMAX, TILE):
             rows = slice(at, at + TILE)
             weights = weights_ref[0, head, rows, :]
-            weight_grad = mm_nt(cotangent[rows], values)
+            cotangent = cg_ref[order_ref[at // TILE], 0, :, part]
+            weight_grad = mm_nt(cotangent, values)
             inner = jnp.sum(weights * weight_grad, axis=-1, keepdims=True)
             score_grad = (weights * (weight_grad - inner) * score_factor()).astype(BF16)
             ds_ref[rows, :] = score_grad
-            value_grad = value_grad + mm_tn(weights.astype(BF16), cotangent[rows])
+            value_grad = value_grad + mm_tn(weights.astype(BF16), cotangent)
             by_offset = unskew(flipped(score_grad)).astype(BF16)
             window = window_of(at)
             query_grad = mm(score_grad, keys) + mm_nt(by_offset, pk_back_ref[part, window])
@@ -260,7 +261,8 @@
     total = mm_nt(rows_ref[:, :local], wq_ref[...])
     total = total + mm_nt(rows_ref[:, local : 2 * local], wk_ref[...])
     total = total + mm_nt(rows_ref[:, 2 * local :], wv_ref[...])
-    part_ref[...] = total.astype(BF16)
+    for at in range(0, SEQMAX, TILE):
+        part_ref[at // TILE, 0] = total[at : at + TILE].astype(BF16)
     sum_ref[...] += mm_tn(hidden_ref[...], rows_ref[...])
 
     @pl.when(block == blocks - 1)
@@ -289,7 +291,7 @@
 
 
 def backward_attention(
-    context_grad, queries, keys, values, weights, pk_back, pq_back,
+    order, context_grad, queries, keys, values, weights, pk_back, pq_back,
     hidden, w_query, w_key, w_value, table, rel_rows, kind,
 ):
     tokens, width = hidden.shape
@@ -297,6 +299,7 @@
     heads = local // HEAD_DIM
     buckets = table.shape[0]
     blocks = tokens // SEQMAX
+    groups = SEQMAX // TILE
     whole = lambda *shape: pl.BlockSpec(shape, lambda b: (0,) * len(shape))
     rows = lambda w: pl.BlockSpec((SEQMAX, w), lambda b: (b, 0))
     shape = jax.ShapeDtypeStruct
@@ -304,7 +307,8 @@
         backward_kernel,
         grid=(blocks,),
         in_specs=[
-            rows(local),
+            pl.BlockSpec(memory_space=pltpu.SMEM),
+            pl.BlockSpec((groups, 1, TILE, local), lambda b: (0, b, 0, 0)),
             rows(local),
             rows(local),
             rows(local),
@@ -318,9 +322,13 @@
             whole(buckets, width),
             whole(2, OFFSETS),
         ],
-        out_specs=[rows(width), whole(width, 3 * local), whole(buckets, 2 * local)],
+        out_specs=[
+            pl.BlockSpec((groups, 1, TILE, width), lambda b: (0, b, 0, 0)),
+            whole(width, 3 * local),
+            whole(buckets, 2 * local),
+        ],
         out_shape=[
-            shape((tokens, width), BF16),
+            shape((groups, blocks, TILE, width), BF16),
             shape((width, 3 * local), kind),
             shape((buckets, 2 * local), kind),
         ],
@@ -339,7 +347,7 @@
         ),
         name="attention_backward",
     )(
-        context_grad, queries, keys, values, weights, pk_back, pq_back,
+        order, context_grad, queries, keys, values, weights, pk_back, pq_back,
         hidden, w_query, w_key, w_value, table, rel_rows,
     )
 
@@ -350,26 +358,246 @@
     return jnp.stack([plain, back])
 
 
-def exact_dot(left, right):
-    return jnp.dot(left, right, precision=lax.Precision.HIGHEST, preferred_element_type=F32)
-
-
-def float_dot(left, right):
-    return jnp.dot(left, right, preferred_element_type=F32)
-
-
-def layer_norm(resid, gain, offset):
-    average = jnp.mean(resid, axis=-1, keepdims=True)
-    centered = resid - average
-    variance = jnp.mean(centered * centered, axis=-1, keepdims=True)
-    return centered * lax.rsqrt(variance + NORM_EPS) * gain + offset
-
-
-def exact_gelu(pre_act):
-    return jax.nn.gelu(pre_act, approximate=False)
+CHUNKS = 8
+PAD_ROWS = 64
+
+
+def layer_norm_parts(resid):
+    centered = resid - jnp.mean(resid, axis=-1, keepdims=True)
+    scale = lax.rsqrt(jnp.mean(centered * centered, axis=-1, keepdims=True) + NORM_EPS)
+    return centered * scale, scale
+
+
+def layer_norm_back(normal, scale, grad, gain):
+    inner = grad * gain
+    mean = jnp.mean(inner, axis=-1, keepdims=True)
+    along = jnp.mean(inner * normal, axis=-1, keepdims=True)
+    return scale * (inner - mean - normal * along)
+
+
+def token_kernel(
+    order_ref, context_ref, hidden_ref, out_grad_ref, norms_ref, packed_ref,
+    output_ref, context_grad_ref, resid_ref, first_low_ref, act_ref, pre_grad_ref, ffn_grad_ref,
+    attn_grad_ref, norm_grads_ref,
+    packed_vmem, slope_ref, sems,
+):
+    groups = packed_vmem.shape[0]
+    width = hidden_ref.shape[1]
+    hidden_units = act_ref.shape[2]
+    local = context_ref.shape[2]
+    copies = [
+        pltpu.make_async_copy(packed_ref.at[:, g], packed_vmem.at[g], sems.at[g])
+        for g in range(groups)
+    ]
+    for copy in copies:
+        copy.start()
+
+    def packed(g):
+        return packed_vmem[g].reshape(-1, width)
+
+    def w_in(g):
+        return packed(g)[:width]
+
+    def w_down(g):
+        return packed(g)[width : width + hidden_units]
+
+    def w_out(g):
+        return packed(g)[width + hidden_units : width + hidden_units + local]
+
+    for copy in copies:
+        copy.wait()
+    gain_one, bias_one = norms_ref[0:1, :], norms_ref[1:2, :]
+    gain_two, bias_two = norms_ref[2:3, :], norms_ref[3:4, :]
+    resid = hidden_ref[...].astype(F32)
+    for g in range(groups):
+        resid = resid + mm(context_ref[order_ref[g]], w_out(g)).astype(BF16).astype(F32)
+    normal_one, scale_one = layer_norm_parts(resid)
+    first_norm = normal_one * gain_one + bias_one
+    first_low = first_norm.astype(BF16)
+    first_low_ref[...] = first_low
+    ffn_out = first_norm
+    for g in range(groups):
+        pre_act = mm(first_low, w_in(g))
+        area = 0.5 * (1.0 + lax.erf(pre_act * math.sqrt(0.5)))
+        activated = (pre_act * area).astype(BF16)
+        act_ref[g] = activated
+        density = jnp.exp(-0.5 * pre_act * pre_act) * (1.0 / math.sqrt(2.0 * math.pi))
+        slope_ref[g] = area + pre_act * density
+        ffn_out = ffn_out + mm(activated, w_down(g)).astype(BF16).astype(F32)
+    normal_two, scale_two = layer_norm_parts(ffn_out)
+    output_ref[...] = (normal_two * gain_two + bias_two).astype(BF16)
+    out_grad = out_grad_ref[...].astype(F32)
+    norm_grads_ref[...] = jnp.zeros_like(norm_grads_ref)
+    norm_grads_ref[2:3, :] = jnp.sum(out_grad * normal_two, axis=0, keepdims=True)
+    norm_grads_ref[3:4, :] = jnp.sum(out_grad, axis=0, keepdims=True)
+    second_grad = layer_norm_back(normal_two, scale_two, out_grad, gain_two)
+    ffn_grad = second_grad.astype(BF16)
+    ffn_grad_ref[...] = ffn_grad
+    first_grad = second_grad
+    for g in range(groups):
+        pre_grad = (mm_nt(ffn_grad, w_down(g)) * slope_ref[g]).astype(BF16)
+        pre_grad_ref[g] = pre_grad
+        first_grad = first_grad + mm_nt(pre_grad, w_in(g))
+    norm_grads_ref[0:1, :] = jnp.sum(first_grad * normal_one, axis=0, keepdims=True)
+    norm_grads_ref[1:2, :] = jnp.sum(first_grad, axis=0, keepdims=True)
+    resid_grad = layer_norm_back(normal_one, scale_one, first_grad, gain_one)
+    resid_ref[...] = resid_grad
+    attn_grad = resid_grad.astype(BF16)
+    attn_grad_ref[...] = attn_grad
+    for g in range(groups):
+        context_grad_ref[g] = mm_nt(attn_grad, w_out(g)).astype(BF16)
+
+
+def token_layer(order, context, hidden, out_grad, norms, packed):
+    chunks, groups, chunk_rows, width = packed.shape
+    tokens = hidden.shape[0]
+    local = context.shape[2]
+    units = chunks * chunk_rows - PAD_ROWS - local - width
+    shape = jax.ShapeDtypeStruct
+    vmem = pl.BlockSpec(memory_space=pltpu.VMEM)
+    return pl.pallas_call(
+        token_kernel,
+        in_specs=[pl.BlockSpec(memory_space=pltpu.SMEM)]
+        + [vmem] * 4
+        + [pl.BlockSpec(memory_space=pl.ANY)],
+        out_specs=[vmem] * 9,
+        out_shape=[
+            shape((tokens, width), BF16),
+            shape((groups, tokens, local), BF16),
+            shape((tokens, width), F32),
+            shape((tokens, width), BF16),
+            shape((groups, tokens, units), BF16),
+            shape((groups, tokens, units), BF16),
+            shape((tokens, width), BF16),
+            shape((tokens, width), BF16),
+            shape((8, width), F32),
+        ],
+        scratch_shapes=[
+            pltpu.VMEM((groups, chunks, chunk_rows, width), BF16),
+            pltpu.VMEM((groups, tokens, units), F32),
+            pltpu.SemaphoreType.DMA((groups,)),
+        ],
+        compiler_params=pltpu.CompilerParams(vmem_limit_bytes=48 * 2**20),
+        cost_estimate=pl.CostEstimate(
+            flops=5_000_000_000, bytes_accessed=18_000_000, transcendentals=1_600_000
+        ),
+        name="token_layer",
+    )(order, context, hidden, out_grad, norms, packed)
+
+
+def weight_grad_kernel(
+    order_ref, context_ref, first_low_ref, act_ref, pre_grad_ref, ffn_grad_ref, attn_grad_ref,
+    out_ref,
+):
+    whole = jnp.concatenate(
+        [
+            mm_tn(first_low_ref[...], pre_grad_ref[0]),
+            mm_tn(act_ref[0], ffn_grad_ref[...]),
+            mm_tn(context_ref[0], attn_grad_ref[...]),
+            jnp.zeros((PAD_ROWS, first_low_ref.shape[1]), F32),
+        ],
+        axis=0,
+    ).astype(BF16)
+    rows = out_ref.shape[2]
+    for chunk in range(out_ref.shape[0]):
+        out_ref[chunk, 0] = whole[chunk * rows : (chunk + 1) * rows]
+
+
+def weight_grads(order, context, first_low, act, pre_grad, ffn_grad, attn_grad):
+    groups, tokens, units = act.shape
+    width = first_low.shape[1]
+    local = context.shape[2]
+    rows = (width + units + local + PAD_ROWS) // CHUNKS
+    whole = lambda *shape: pl.BlockSpec(shape, lambda g, order: (0,) * len(shape))
+    group = lambda w: pl.BlockSpec((1, tokens, w), lambda g, order: (g, 0, 0))
+    return pl.pallas_call(
+        weight_grad_kernel,
+        grid_spec=pltpu.PrefetchScalarGridSpec(
+            num_scalar_prefetch=1,
+            grid=(groups,),
+            in_specs=[
+                pl.BlockSpec((1, tokens, local), lambda g, order: (order[g], 0, 0)),
+                whole(tokens, width),
+                group(units),
+                group(units),
+                whole(tokens, width),
+                whole(tokens, width),
+            ],
+            out_specs=pl.BlockSpec((CHUNKS, 1, rows, width), lambda g, order: (0, g, 0, 0)),
+        ),
+        out_shape=jax.ShapeDtypeStruct((CHUNKS, groups, rows, width), BF16),
+        compiler_params=pltpu.CompilerParams(
+            dimension_semantics=("arbitrary",), vmem_limit_bytes=40 * 2**20
+        ),
+        cost_estimate=pl.CostEstimate(
+            flops=2_800_000_000, bytes_accessed=14_000_000, transcendentals=0
+        ),
+        name="weight_grads",
+    )(order, context, first_low, act, pre_grad, ffn_grad, attn_grad)
+
+
+def place_kernel(order_ref, *refs):
+    out_ref = refs[-1]
+    for shift, piece_ref in enumerate(refs[:-1]):
+        out_ref[:, order_ref[shift]] = piece_ref[...].reshape(out_ref.shape[0], TILE, -1)
+
+
+def place(order, pieces):
+    rows, width = pieces[0].shape
+    blocks = rows // TILE
+    vmem = pl.BlockSpec(memory_space=pltpu.VMEM)
+    out = pl.pallas_call(
+        place_kernel,
+        in_specs=[pl.BlockSpec(memory_space=pltpu.SMEM)] + [vmem] * len(pieces),
+        out_specs=vmem,
+        out_shape=jax.ShapeDtypeStruct((blocks, len(pieces), TILE, width), BF16),
+        cost_estimate=pl.CostEstimate(flops=0, bytes_accessed=3_000_000, transcendentals=0),
+        name="place",
+    )(order, *pieces)
+    return out.reshape(rows * len(pieces), width)
+
+
+def send(array, shift, size):
+    return lax.ppermute(array, "tensor", [(i, (i + shift) % size) for i in range(size)])
+
+
+def exchange(array, me, size):
+    pick = lambda s: lax.dynamic_index_in_dim(array, (me + s) % size, 0, keepdims=False)
+    return [pick(0)] + [send(pick(s), s, size) for s in range(1, size)]
+
+
+def spread(array, size):
+    return [array] + [send(array, s, size) for s in range(1, size)]
+
+
+def halve(array, axis_index, bits):
+    size = 2 ** len(bits)
+    for bit in bits:
+        half = array.shape[0] // 2
+        mine = (axis_index >> bit) & 1
+        keep = lax.dynamic_slice_in_dim(array, mine * half, half, 0)
+        give = lax.dynamic_slice_in_dim(array, (1 - mine) * half, half, 0)
+        pairs = [(i, i ^ (1 << bit)) for i in range(size)]
+        got = lax.ppermute(give, "dp", pairs)
+        array = (keep.astype(F32) + got.astype(F32)).astype(BF16)
+    return array
+
+
+def double(array, axis_index, bits):
+    size = 2 ** len(bits)
+    for bit in bits[::-1]:
+        pairs = [(i, i ^ (1 << bit)) for i in range(size)]
+        got = lax.ppermute(array, "dp", pairs)
+        low = (axis_index >> bit) & 1 == 0
+        array = jnp.where(
+            low, jnp.concatenate([array, got], 0), jnp.concatenate([got, array], 0)
+        )
+    return array
 
 
 def shards(
+    n_dp,
+    n_tensor,
     hidden,
     out_grad,
     w_query,
@@ -387,119 +615,101 @@
     group_counts,
     key_mask,
 ):
-    local_width = w_query.shape[1]
+    tokens, width = hidden.shape
+    local = w_query.shape[1]
+    units = w_in.shape[1]
+    buckets = bucket_table.shape[0]
+    blocks = tokens // SEQMAX
+    mine = tokens // n_tensor
+    replica = lax.axis_index("dp")
+    me = lax.axis_index("tensor")
+    order = (me - jnp.arange(n_tensor, dtype=jnp.int32)) % n_tensor
     rel_rows = offset_rows(rel_buckets)
+
+    packed = jnp.concatenate([w_in, w_down, w_out, jnp.zeros((PAD_ROWS, width), BF16)], 0)
+    chunk_rows = packed.shape[0] // CHUNKS
+    if n_dp == CHUNKS:
+        piece = lax.dynamic_slice_in_dim(packed, replica * chunk_rows, chunk_rows, 0)
+        packed = lax.all_gather(piece, ("dp", "tensor"), axis=0, tiled=False)
+        packed = packed.reshape(CHUNKS, n_tensor, chunk_rows, width)
+    else:
+        packed = lax.all_gather(packed, "tensor", axis=0, tiled=False)
+        packed = packed.reshape(n_tensor, CHUNKS, chunk_rows, width).swapaxes(0, 1)
+
+    def my_rows(array):
+        array = array.reshape(blocks, n_tensor, TILE, width)
+        return lax.dynamic_index_in_dim(array, me, 1, keepdims=False).reshape(mine, width)
+
     query_rows, key_rows, value_rows, weights, context, pk_back, pq_back = forward_attention(
         hidden, w_query, w_key, w_value, bucket_table, rel_rows, group_counts, key_mask
     )
-    attn_out = lax.psum(float_dot(context, w_out).astype(jnp.bfloat16), "tensor").astype(
-        jnp.float32
+    pieces = context.reshape(blocks, n_tensor, TILE, local).swapaxes(0, 1)
+    pieces = pieces.reshape(n_tensor, mine, local)
+    context = jnp.stack(exchange(pieces, me, n_tensor))
+    norms = jnp.stack([gain_one, bias_one, gain_two, bias_two])
+    (
+        output, context_grad, resid_grad, first_low, act, pre_grad, ffn_grad, attn_grad, norm_grads,
+    ) = token_layer(order, context, my_rows(hidden), my_rows(out_grad), norms, packed)
+    context_grad = jnp.stack(exchange(context_grad, me, n_tensor))
+    context_grad = context_grad.reshape(n_tensor, blocks, TILE, local)
+    output = place(order, spread(output, n_tensor))
+    grads = weight_grads(order, context, first_low, act, pre_grad, ffn_grad, attn_grad)
+    if n_dp == CHUNKS:
+        grads = lax.psum_scatter(grads, "dp", scatter_dimension=0, tiled=True)
+        grads = lax.psum_scatter(grads[0], "tensor", scatter_dimension=0, tiled=True)
+        grads = lax.all_gather(grads[0], "dp", axis=0, tiled=True)
+    else:
+        grads = grads.swapaxes(0, 1).reshape(n_tensor, CHUNKS * chunk_rows, width)
+        grads = lax.psum_scatter(grads, "tensor", scatter_dimension=0, tiled=True)
+        grads = lax.psum(grads[0], "dp")
+
+    hidden_part, row_grads, pos_grads = backward_attention(
+        order, context_grad, query_rows, key_rows, value_rows, weights, pk_back, pq_back,
+        hidden, w_query, w_key, w_value, bucket_table, rel_rows, BF16,
     )
-    first_norm, norm_one_back = jax.vjp(
-        layer_norm, hidden.astype(jnp.float32) + attn_out, gain_one, bias_one
-    )
-    first_low = first_norm.astype(jnp.bfloat16)
-    pre_act = float_dot(first_low, w_in)
-    activated_full, gelu_back = jax.vjp(exact_gelu, pre_act)
-    activated = activated_full.astype(jnp.bfloat16)
-    ffn_out = lax.psum(float_dot(activated, w_down).astype(jnp.bfloat16), "tensor").astype(
-        jnp.float32
-    )
-    second_norm, norm_two_back = jax.vjp(layer_norm, first_norm + ffn_out, gain_two, bias_two)
-    output = second_norm.astype(jnp.bfloat16)
-    second_grad, grad_gain_two, grad_bias_two = norm_two_back(out_grad.astype(jnp.float32))
-    ffn_grad = second_grad.astype(jnp.bfloat16)
-    down_local = jnp.einsum("tf,td->fd", activated, ffn_grad, preferred_element_type=jnp.float32)
-    act_grad = jnp.einsum("td,fd->tf", ffn_grad, w_down, preferred_element_type=jnp.float32)
-    pre_grad = gelu_back(act_grad)[0].astype(jnp.bfloat16)
-    in_local = jnp.einsum("tc,tf->cf", first_low, pre_grad, preferred_element_type=jnp.float32)
-    back_part = jnp.einsum("tf,cf->tc", pre_grad, w_in, preferred_element_type=jnp.float32)
-    first_grad = second_grad + lax.psum(back_part.astype(jnp.bfloat16), "tensor").astype(
-        jnp.float32
-    )
-    resid_grad, grad_gain_one, grad_bias_one = norm_one_back(first_grad)
-    attn_grad = resid_grad.astype(jnp.bfloat16)
-    out_local = jnp.einsum("tk,td->kd", context, attn_grad, preferred_element_type=jnp.float32)
-    context_grad = jnp.einsum(
-        "td,kd->tk", attn_grad, w_out, preferred_element_type=jnp.float32
-    ).astype(jnp.bfloat16)
-
-    hidden_part, local_grads, pos_grads = backward_attention(
-        context_grad, query_rows, key_rows, value_rows, weights, pk_back, pq_back,
-        hidden, w_query, w_key, w_value, bucket_table, rel_rows, F32,
-    )
-    grad_hidden = (
-        resid_grad + lax.psum(hidden_part.astype(jnp.bfloat16), "tensor").astype(jnp.float32)
-    ).astype(jnp.bfloat16)
-    query_local = local_grads[:, :local_width]
-    key_local = local_grads[:, local_width : 2 * local_width]
-    value_local = local_grads[:, 2 * local_width :]
-    key_wide = w_key.astype(jnp.float32)
-    query_wide = w_query.astype(jnp.float32)
-    table_part = exact_dot(pos_grads[:, :local_width], key_wide.T)
-    table_part = table_part + exact_dot(pos_grads[:, local_width:], query_wide.T)
-    shares = (
-        lax.psum_scatter(query_local, "dp", scatter_dimension=0, tiled=True),
-        lax.psum_scatter(key_local, "dp", scatter_dimension=0, tiled=True),
-        lax.psum_scatter(value_local, "dp", scatter_dimension=0, tiled=True),
-        lax.psum_scatter(out_local, "dp", scatter_dimension=1, tiled=True),
-        lax.psum_scatter(in_local, "dp", scatter_dimension=0, tiled=True),
-        lax.psum_scatter(down_local, "dp", scatter_dimension=1, tiled=True),
-        lax.psum_scatter(grad_gain_one, "dp", scatter_dimension=0, tiled=True),
-        lax.psum_scatter(grad_bias_one, "dp", scatter_dimension=0, tiled=True),
-        lax.psum_scatter(grad_gain_two, "dp", scatter_dimension=0, tiled=True),
-        lax.psum_scatter(grad_bias_two, "dp", scatter_dimension=0, tiled=True),
-    )
-    gathered = (
-        lax.all_gather(shares[0].astype(jnp.bfloat16), "dp", axis=0, tiled=True).astype(
-            jnp.float32
-        ),
-        lax.all_gather(shares[1].astype(jnp.bfloat16), "dp", axis=0, tiled=True).astype(
-            jnp.float32
-        ),
-        lax.all_gather(shares[2].astype(jnp.bfloat16), "dp", axis=0, tiled=True).astype(
-            jnp.float32
-        ),
-        lax.all_gather(shares[3].astype(jnp.bfloat16), "dp", axis=1, tiled=True).astype(
-            jnp.float32
-        ),
-        lax.all_gather(shares[4].astype(jnp.bfloat16), "dp", axis=0, tiled=True).astype(
-            jnp.float32
-        ),
-        lax.all_gather(shares[5].astype(jnp.bfloat16), "dp", axis=1, tiled=True).astype(
-            jnp.float32
-        ),
-        lax.all_gather(shares[6].astype(jnp.bfloat16), "dp", axis=0, tiled=True).astype(
-            jnp.float32
-        ),
-        lax.all_gather(shares[7].astype(jnp.bfloat16), "dp", axis=0, tiled=True).astype(
-            jnp.float32
-        ),
-        lax.all_gather(shares[8].astype(jnp.bfloat16), "dp", axis=0, tiled=True).astype(
-            jnp.float32
-        ),
-        lax.all_gather(shares[9].astype(jnp.bfloat16), "dp", axis=0, tiled=True).astype(
-            jnp.float32
-        ),
-    )
-    grad_query = gathered[0]
-    grad_key = gathered[1]
-    table_share = lax.psum_scatter(table_part, ("dp", "tensor"), scatter_dimension=0, tiled=True)
-    grad_table = lax.all_gather(table_share, ("dp", "tensor"), axis=0, tiled=True)
+    got = exchange(hidden_part.reshape(n_tensor, mine, width), me, n_tensor)
+    grad_hidden = resid_grad
+    for piece in got:
+        grad_hidden = grad_hidden + piece.astype(F32)
+    grad_hidden = place(order, spread(grad_hidden.astype(BF16), n_tensor))
+
+    pos_rows, row_rows = buckets // n_dp, width // n_dp
+    norm_cols = 4 * width // n_dp
+    pos_grads = pos_grads.reshape(n_dp, pos_rows, 2 * local)
+    norm_grads = norm_grads[:4].reshape(n_dp, 1, norm_cols).astype(BF16)
+    norm_grads = jnp.pad(norm_grads, ((0, 0), (0, 0), (0, 2 * local - norm_cols)))
+    pos_grads = jnp.concatenate([pos_grads, norm_grads], 1)
+    pos_grads = jnp.pad(pos_grads, ((0, 0), (0, row_rows - pos_rows - 1), (0, 0)))
+    joined = jnp.concatenate([pos_grads.reshape(width, 2 * local), row_grads], 1)
+    bits = list(range(n_dp.bit_length() - 1))
+    joined = halve(joined, replica, bits)
+    table_part = mm_nt(joined[:pos_rows, : 2 * local], jnp.concatenate([w_key, w_query], 1))
+    norm_part = jnp.pad(joined[pos_rows : pos_rows + 1, :norm_cols], ((0, 0), (0, width - norm_cols)))
+    share = jnp.concatenate([table_part.astype(BF16), norm_part], 0)
+    share = jnp.pad(share, ((0, row_rows - pos_rows - 1), (0, 0)))
+    shares = jnp.stack(spread(share, n_tensor)).astype(F32)
+    in_order = [lax.dynamic_index_in_dim(shares, order[g], 0, False) for g in range(n_tensor)]
+    share = sum(in_order).astype(BF16)
+    joined = double(jnp.concatenate([share, joined[:, 2 * local :]], 1), replica, bits)
+    small = joined[:, :width].reshape(n_dp, row_rows, width).astype(F32)
+    grad_table = small[:, :pos_rows].reshape(buckets, width)
+    norm_grads = small[:, pos_rows, :norm_cols].reshape(4, width)
+    row_grads = joined[:, width:].astype(F32)
+    grads = grads.astype(F32)
     return (
         output,
         grad_hidden,
-        grad_query,
-        grad_key,
-        gathered[2],
-        gathered[3],
-        gathered[4],
-        gathered[5],
+        row_grads[:, :local],
+        row_grads[:, local : 2 * local],
+        row_grads[:, 2 * local :],
+        grads[width + units : width + units + local],
+        grads[:width],
+        grads[width : width + units],
         grad_table,
-        gathered[6],
-        gathered[7],
-        gathered[8],
-        gathered[9],
+        norm_grads[0],
+        norm_grads[1],
+        norm_grads[2],
+        norm_grads[3],
     )
 
 
@@ -537,4 +747,5 @@
         P(),
         P(),
     )
-    return jax.shard_map(shards, mesh=mesh, in_specs=in_specs, out_specs=out_specs, check_vma=False)
+    body = functools.partial(shards, mesh.shape["dp"], mesh.shape["tensor"])
+    return jax.shard_map(body, mesh=mesh, in_specs=in_specs, out_specs=out_specs, check_vma=False)

time: 833 us -> 454 us (0.55)
  waiting for transfers between devices: 549 us -> 220 us
  blocking collectives: 76.8 us -> 0 us
  starting transfers between devices: 13.5 us -> 63.5 us
  matrix products: 36.7 us -> 0.21 us
  Pallas kernels: 51.6 us -> 75.3 us
  other arithmetic: 32.9 us -> 17.1 us
    psum x4 -> x0, waiting for transfers between devices: 241 us -> none  [the longest x1 68.3 us: shards(): lax.psum(float_dot(activated, w_down).astype(jnp.bfloat16), 'tensor')]
    reduce_scatter x6 -> x2, waiting for transfers between devices: 206 us -> 67.8 us  [the longest x1 67.8 us: shards(): grads = lax.psum_scatter(grads, 'dp', scatter_dimension=0, tiled=True)]
    ppermute x0 -> x24, waiting for transfers between devices: none -> 105 us  [the longest x18 83.9 us: send(): lax.ppermute(array, 'tensor', [(i, (i + shift) % size) for i in range(siz...]
    ppermute x0 -> x24, starting transfers between devices: none -> 63.3 us  [the longest x18 54.1 us: send(): lax.ppermute(array, 'tensor', [(i, (i + shift) % size) for i in range(siz...]
    all_gather x3 -> x2, waiting for transfers between devices: 99.8 us -> 47.8 us  [the longest x1 47.8 us: shards(): packed = lax.all_gather(piece, ('dp', 'tensor'), axis=0, tiled=False)]
    all_gather x4 -> x0, blocking collectives: 42.5 us -> none  [the longest x1 11.6 us: shards(): lax.all_gather(shares[3].astype(jnp.bfloat16), 'dp', axis=1, tiled=True)]
    unnamed x2 -> x0, blocking collectives: 34.3 us -> none
    dot_general x10 -> x1, matrix products: 33 us -> 0.21 us  [mm_nt(): lax.dot_general(left, right, (((1,), (1,)), ((), ())), preferred_element_...]
  transfers between devices with their start and end apart: 14 -> 28, of which waited for: 12 -> 13; matrix products, arithmetic and copies ran while one was open for 6% -> 9% of each run, Pallas kernels for 4% -> 13%
where the time goes in v1:
time: 454 us; the launch traced here: 446 us
  waiting for transfers between devices  220 us (48%)
  Pallas kernels  75.3 us (17%)
  starting transfers between devices  63.5 us (14%)
  local copies, waits for them, and re-layouts  47.6 us (10%)
  between operations  22.6 us (5%)
  other arithmetic  17.1 us (4%)
    ppermute x18, waiting for transfers between devices, send(): lax.ppermute(array, 'tensor', [(i, (i + shift) % size) for i in range(siz...  83.9 us
    reduce_scatter x1, waiting for transfers between devices, shards(): grads = lax.psum_scatter(grads, 'dp', scatter_dimension=0, tiled=True)  67.8 us
    ppermute x18, starting transfers between devices, send(): lax.ppermute(array, 'tensor', [(i, (i + shift) % size) for i in range(siz...  54.1 us
    all_gather x1, waiting for transfers between devices, shards(): packed = lax.all_gather(piece, ('dp', 'tensor'), axis=0, tiled=False)  47.8 us
    pallas_call x1, Pallas kernels, backward_attention(): pl.pallas_call(backward_kernel, grid=(blocks,), in_specs=[pl.BlockSpec(me...  32.4 us
    unnamed x82, local copies, waits for them, and re-layouts  21.8 us
    pallas_call x1, Pallas kernels, forward_attention(): pl.pallas_call(forward_kernel, grid=(blocks,), in_specs=[rows(width), who...  18.9 us
    ppermute x3, waiting for transfers between devices, halve(): got = lax.ppermute(give, 'dp', pairs)  15.5 us
  transfers between devices with their start and end apart: 28, of which 13 were waited for; matrix products, arithmetic and copies ran while one was open for 9% of the time, Pallas kernels for 13%

profile of v1, /device:TPU:31, one launch (start us, length us, event | category | flops | bytes accessed | tf_op | source)
XLA Modules:
  0.0 446.4 jit_solution(17964807163357758976)
XLA Ops:
  13.4 18.9 %attention_forward.1 = (bf16[1024,192]{1,0:T(8,128)(2,1)S(1)}, bf16[1024,192]{1,0:T(8,128)(2,1)S(1)}, bf16[1024,192]{1,0:T(8,128)(2,1)S(1)}, f32[2,3,512,512]{3,...) custom-call(bf16[1024,768]{1,0:T(8,128)(2,1)S(1)} %copy-done.4, ...), custom_call_target="tpu_custom_call" | custom-call | flops 8000000000 | bytes 12000000 | tf_op jit(solution)/shard_map/attention_forward/pallas_call | solution.py:159
  32.3 2.6 copy-done.10
  40.9 3.2 collective-permute-start
  46.1 13.4 %collective-permute-done.1 = bf16[256,192]{1,0:T(8,128)(2,1)} collective-permute-done((bf16[256,192]{1,0:T(8,128)(2,1)}, bf16[256,192]{1,0:T(8,128)(2,1)}, u32[]{:S(2)}, u32[]{:S(2)}) %collective-permute-start.1) | collective-permute-done | bytes 98336 | tf_op jit(solution)/shard_map/ppermute | solution.py:561
  60.7 47.8 %all-gather.5.cloned.1.call-done = bf16[7168,768]{1,0:T(8,128)(2,1)} async-done(((bf16[224,768]{1,0:T(8,128)(2,1)}), bf16[7168,768]{1,0:T(8,128)(2,1)}) %all-gather.5.cloned.1.call-update) | async-done | bytes 11010064 | tf_op jit(solution)/shard_map/all_gather | solution.py:633
  109.5 12.4 %token_layer.1 = (bf16[256,768]{1,0:T(8,128)(2,1)S(1)}, bf16[4,256,192]{2,1,0:T(8,128)(2,1)S(1)}, f32[256,768]{1,0:T(8,128)S(1)}, bf16[256,768]{1,0:T(8,128)(2,1...) custom-call(s32[4]{0:T(128)S(1)} %and_select_fusion.order_ref, ...), custom_call_target="tpu_custom_call" | custom-call | flops 5000000000 | bytes 18000000 | tf_op jit(solution)/shard_map/token_layer/pallas_call | solution.py:458
  124.0 6.4 %weight_grads.1 = bf16[8,4,224,768]{3,2,1,0:T(8,128)(2,1)} custom-call(s32[4]{0:T(128)S(1)} %and_select_fusion.order_ref, bf16[4,256,192]{2,1,0:T(8,128)(2,1)S(1)} %pad_maximum_fusion.context_ref, bf16[256,768]{1,0:T(8,128)(2,1)S(1)} %get-tuple-element.46.first_low_ref, bf16[4,256,768]{2,1,0:T(8,128)(2,1)S(1)} %get-tuple-element.47.act_ref, ...), custom_call_target="tpu_custom_call" | custom-call | flops 2800000000 | bytes 14000000 | tf_op jit(solution)/shard_map/weight_grads/pallas_call | solution.py:513
  136.0 9.4 %collective-permute-done.7 = bf16[256,192]{1,0:T(8,128)(2,1)S(1)} collective-permute-done((bf16[256,192]{1,0:T(8,128)(2,1)S(1)}, bf16[256,192]{1,0:T(8,128)(2,1)S(1)}, u32[]{:S(2)}, u32[]{:S(2)}) %collective-permute-start.7) | collective-permute-done | bytes 98336 | tf_op jit(solution)/shard_map/ppermute | solution.py:561
  146.5 67.8 %reduce-scatter.3.cloned.1.call-done = bf16[1,4,224,768]{3,2,1,0:T(8,128)(2,1)} async-done(((bf16[8,4,224,768]{3,2,1,0:T(8,128)(2,1)}), bf16[1,4,224,768]{3,2,1,0:T(8,128)(2,1)}) %reduce-scatter.3.cloned.1.call-update) | async-done | bytes 1376272 | tf_op jit(solution)/shard_map/reduce_scatter | solution.py:658
  219.6 32.4 %attention_backward.1 = (bf16[4,2,128,768]{3,2,1,0:T(8,128)(2,1)}, bf16[768,576]{1,0:T(8,128)(2,1)}, bf16[512,384]{1,0:T(8,128)(2,1)S(1)}) custom-call(s32[4]{0:T(128)S(1)} %and_select_fusion.order_ref, bf16[4,2,128,192]{3,2,1,0:T(8,128)(2,1)S(1)} %pad_maximum_fusion.1.cg_ref, bf16[1024,192]{1,0:T(8,128)(2,1)S(1)} %copy-done.12, ...), custom_call_target="tpu_custom_call" | custom-call | flops 16000000000 | bytes 16000000 | tf_op jit(solution)/shard_map/attention_backward/pallas_call | solution.py:306
  254.2 2.3 copy.52
  257.1 2.2 collective-permute-done.15
  259.3 2.3 copy.53
  261.6 2.2 add_convert_fusion
  266.0 9.3 %collective-permute-done.16 = bf16[192,960]{1,0:T(8,128)(2,1)S(1)} collective-permute-done((bf16[192,960]{1,0:T(8,128)(2,1)S(1)}, bf16[192,960]{1,0:T(8,128)(2,1)S(1)}, u32[]{:S(2)}, u32[]{:S(2)}) %collective-permute-start.16) | collective-permute-done | bytes 368672 | tf_op jit(solution)/shard_map/ppermute | solution.py:581
  277.6 4.1 collective-permute-done.17
  292.2 2.7 collective-permute-done.19
  296.2 5.1 %collective-permute-done.21 = bf16[96,1344]{1,0:T(8,128)(2,1)S(1)} collective-permute-done((bf16[96,1344]{1,0:T(8,128)(2,1)S(1)}, bf16[96,1344]{1,0:T(8,128)(2,1)S(1)}, u32[]{:S(2)}, u32[]{:S(2)}) %collective-permute-start.21) | collective-permute-done | bytes 258080 | tf_op jit(solution)/shard_map/ppermute | solution.py:590
  301.4 3.2 collective-permute-start.22
  304.6 2.3 dynamic-slice_bitcast_fusion.2
  306.8 9.3 %collective-permute-start.10 = (bf16[256,768]{1,0:T(8,128)(2,1)}, bf16[256,768]{1,0:T(8,128)(2,1)}, u32[]{:S(2)}, u32[]{:S(2)}) collective-permute-start(bf16[256,768]{1,0:T(8,128)(2,1)} %get-tuple-element.88), channel_id=1, source_target_pairs={{0,2},{1,3},{2,0},{3,1},{4,6},{5,7},{6,4},{7,5},{8,10},{9,11},{10,... | collective-permute-start | bytes 1179656 | tf_op jit(solution)/shard_map/ppermute | solution.py:561
  316.1 3.3 collective-permute-start.9
  323.2 2.0 collective-permute-start.3
  325.2 17.2 %collective-permute-done.10 = bf16[256,768]{1,0:T(8,128)(2,1)} collective-permute-done((bf16[256,768]{1,0:T(8,128)(2,1)}, bf16[256,768]{1,0:T(8,128)(2,1)}, u32[]{:S(2)}, u32[]{:S(2)}) %collective-permute-start.10) | collective-permute-done | bytes 393248 | tf_op jit(solution)/shard_map/ppermute | solution.py:561
  342.4 19.1 %collective-permute-start.5 = (bf16[256,768]{1,0:T(8,128)(2,1)S(1)}, bf16[256,768]{1,0:T(8,128)(2,1)}, u32[]{:S(2)}, u32[]{:S(2)}) collective-permute-start(bf16[256,768]{1,0:T(8,128)(2,1)S(1)} %copy-done.3), channel_id=1, source_target_pairs={{0,3},{1,0},{2,1},{3,2},{4,7},{5,4},{6,5},{7,6},{8,11},{9,8},{10,9... | collective-permute-start | bytes 1179656 | tf_op jit(solution)/shard_map/ppermute | solution.py:561
  363.2 12.1 %collective-permute-start.13 = (bf16[256,768]{1,0:T(8,128)(2,1)S(1)}, bf16[256,768]{1,0:T(8,128)(2,1)S(1)}, u32[]{:S(2)}, u32[]{:S(2)}) collective-permute-start(bf16[256,768]{1,0:T(8,128)(2,1)S(1)} %fusion.7.refs_0_), channel_id=1, source_target_pairs={{0,2},{1,3},{2,0},{3,1},{4,6},{5,7},{6,4},{7,5},{8,10},{9,11},{10,... | collective-permute-start | bytes 1179656 | tf_op jit(solution)/shard_map/ppermute | solution.py:561
  375.3 17.6 %collective-permute-done.4.refs_2_ = bf16[256,768]{1,0:T(8,128)(2,1)S(1)} collective-permute-done((bf16[256,768]{1,0:T(8,128)(2,1)S(1)}, bf16[256,768]{1,0:T(8,128)(2,1)S(1)}, u32[]{:S(2)}, u32[]{:S(2)}) %collective-permute-start.4) | collective-permute-done | bytes 393248 | tf_op jit(solution)/shard_map/ppermute | solution.py:561
  393.6 2.6 place.2
  396.3 21.9 %collective-permute-done.13.refs_2_ = bf16[256,768]{1,0:T(8,128)(2,1)S(1)} collective-permute-done((bf16[256,768]{1,0:T(8,128)(2,1)S(1)}, bf16[256,768]{1,0:T(8,128)(2,1)S(1)}, u32[]{:S(2)}, u32[]{:S(2)}) %collective-permute-start.13) | collective-permute-done | bytes 393248 | tf_op jit(solution)/shard_map/ppermute | solution.py:561
  418.9 2.6 place.3
  433.9 2.2 convert_element_type.113
  436.1 2.5 slice_bitcast_fusion
  (176 shorter events, 61.7 us)
Async XLA Ops:
  7.2 101.3 %all-gather.5.cloned.1.call-start = ((), (), s32[]{:S(2)}) async-start(), calls=%async_computation.4 | async-start | bytes 11354112 | tf_op jit(solution)/shard_map/all_gather | solution.py:633
  9.4 204.9 %reduce-scatter.3.cloned.1.call-start = ((), (), s32[]{:S(2)}) async-start(), calls=%async_computation.2 | async-start | bytes 12386304 | tf_op jit(solution)/shard_map/reduce_scatter | solution.py:658
  40.7 18.8 %collective-permute-start.1 = (bf16[256,192]{1,0:T(8,128)(2,1)}, bf16[256,192]{1,0:T(8,128)(2,1)}, u32[]{:S(2)}, u32[]{:S(2)}) collective-permute-start(bf16[256,192]{1,0:T(8,128)(2,1)} %get-tuple-element.95), channel_id=1, source_target_pairs={{0,2},{1,3},{2,0},{3,1},{4,6},{5,7},{6,4},{7,5},{8,10},{9,11},{10,... | collective-permute-start | bytes 294920 | tf_op jit(solution)/shard_map/ppermute | solution.py:561
  40.8 18.7 %collective-permute-start.2 = (bf16[256,192]{1,0:T(8,128)(2,1)}, bf16[256,192]{1,0:T(8,128)(2,1)}, u32[]{:S(2)}, u32[]{:S(2)}) collective-permute-start(bf16[256,192]{1,0:T(8,128)(2,1)} %get-tuple-element.94), channel_id=1, source_target_pairs={{0,3},{1,0},{2,1},{3,2},{4,7},{5,4},{6,5},{7,6},{8,11},{9,8},{10,9... | collective-permute-start | bytes 294920 | tf_op jit(solution)/shard_map/ppermute | solution.py:561
  40.9 18.6 %collective-permute-start = (bf16[256,192]{1,0:T(8,128)(2,1)S(1)}, bf16[256,192]{1,0:T(8,128)(2,1)}, u32[]{:S(2)}, u32[]{:S(2)}) collective-permute-start(bf16[256,192]{1,0:T(8,128)(2,1)S(1)} %get-tuple-element.96), channel_id=1, source_target_pairs={{0,1},{1,2},{2,3},{3,0},{4,5},{5,6},{6,7},{7,4},{8,9},{9,10},{10,1... | collective-permute-start | bytes 294920 | tf_op jit(solution)/shard_map/ppermute | solution.py:561
  46.1 237.7 %copy-start.5 = (s32[4]{0:T(128)}, s32[4]{0:T(128)S(1)}, u32[]{:S(2)}) copy-start(s32[4]{0:T(128)S(1)} %and_select_fusion.order_ref) | copy-start | bytes 52
  130.4 147.2 %reduce-scatter.5.cloned.1.call-start = ((), (), s32[]{:S(2)}) async-start(), calls=%async_computation.3 | async-start | bytes 1720320 | tf_op jit(solution)/shard_map/reduce_scatter | solution.py:659
  130.5 83.8 %copy-start.18 = (bf16[192,1024]{1,0:T(8,128)(2,1)S(1)}, bf16[192,1024]{1,0:T(8,128)(2,1)}, u32[]{:S(2)}) copy-start(bf16[192,1024]{1,0:T(8,128)(2,1)} %copy-done.17) | copy-start | bytes 1179652
  131.2 4.8 %collective-permute-start.6 = (bf16[256,192]{1,0:T(8,128)(2,1)S(1)}, bf16[256,192]{1,0:T(8,128)(2,1)S(1)}, u32[]{:S(2)}, u32[]{:S(2)}) collective-permute-start(bf16[256,192]{1,0:T(8,128)(2,1)S(1)} %get-tuple-element.92), channel_id=1, source_target_pairs={{0,1},{1,2},{2,3},{3,0},{4,5},{5,6},{6,7},{7,4},{8,9},{9,10},{10,1... | collective-permute-start | bytes 294920 | tf_op jit(solution)/shard_map/ppermute | solution.py:561
  133.0 12.4 %collective-permute-start.7 = (bf16[256,192]{1,0:T(8,128)(2,1)S(1)}, bf16[256,192]{1,0:T(8,128)(2,1)S(1)}, u32[]{:S(2)}, u32[]{:S(2)}) collective-permute-start(bf16[256,192]{1,0:T(8,128)(2,1)S(1)} %get-tuple-element.91), channel_id=1, source_target_pairs={{0,2},{1,3},{2,0},{3,1},{4,6},{5,7},{6,4},{7,5},{8,10},{9,11},{10,... | collective-permute-start | bytes 294920 | tf_op jit(solution)/shard_map/ppermute | solution.py:561
  133.6 11.8 %collective-permute-start.8 = (bf16[256,192]{1,0:T(8,128)(2,1)S(1)}, bf16[256,192]{1,0:T(8,128)(2,1)S(1)}, u32[]{:S(2)}, u32[]{:S(2)}) collective-permute-start(bf16[256,192]{1,0:T(8,128)(2,1)S(1)} %get-tuple-element.90), channel_id=1, source_target_pairs={{0,3},{1,0},{2,1},{3,2},{4,7},{5,4},{6,5},{7,6},{8,11},{9,8},{10,9... | collective-permute-start | bytes 294920 | tf_op jit(solution)/shard_map/ppermute | solution.py:561
  214.3 219.6 %all-gather.7.cloned.1.call-start = ((), (), s32[]{:S(2)}) async-start(), calls=%async_computation.5 | async-start | bytes 3096576 | tf_op jit(solution)/shard_map/all_gather | solution.py:660
  256.4 2.8 collective-permute-start.15
  264.9 10.4 %collective-permute-start.16 = (bf16[192,960]{1,0:T(8,128)(2,1)S(1)}, bf16[192,960]{1,0:T(8,128)(2,1)S(1)}, u32[]{:S(2)}, u32[]{:S(2)}) collective-permute-start(bf16[192,960]{1,0:T(8,128)(2,1)S(1)} %constant_dynamic-slice_fusion.1), channel_id=1, source_target_pairs={{0,8},{4,12},{8,0},{12,4},{16,24},{20,28},{24,16},{28,20},{1,9},{5... | collective-permute-start | bytes 1105928 | tf_op jit(solution)/shard_map/ppermute | solution.py:581
  276.4 5.3 %collective-permute-start.17 = (bf16[96,960]{1,0:T(8,128)(2,1)S(1)}, bf16[96,960]{1,0:T(8,128)(2,1)S(1)}, u32[]{:S(2)}, u32[]{:S(2)}) collective-permute-start(bf16[96,960]{1,0:T(8,128)(2,1)S(1)} %constant_dynamic-slice_fusion), channel_id=1, source_target_pairs={{0,16},{4,20},{8,24},{12,28},{16,0},{20,4},{24,8},{28,12},{1,17},{... | collective-permute-start | bytes 552968 | tf_op jit(solution)/shard_map/ppermute | solution.py:581
  282.1 10.1 %collective-permute-start.18 = (bf16[96,768]{1,0:T(8,128)(2,1)S(1)}, bf16[96,768]{1,0:T(8,128)(2,1)S(1)}, u32[]{:S(2)}, u32[]{:S(2)}) collective-permute-start(bf16[96,768]{1,0:T(8,128)(2,1)S(1)} %get-tuple-element.98), channel_id=1, source_target_pairs={{0,1},{1,2},{2,3},{3,0},{4,5},{5,6},{6,7},{7,4},{8,9},{9,10},{10,1... | collective-permute-start | bytes 442376 | tf_op jit(solution)/shard_map/ppermute | solution.py:561
  282.3 12.6 %collective-permute-start.19 = (bf16[96,768]{1,0:T(8,128)(2,1)S(1)}, bf16[96,768]{1,0:T(8,128)(2,1)S(1)}, u32[]{:S(2)}, u32[]{:S(2)}) collective-permute-start(bf16[96,768]{1,0:T(8,128)(2,1)S(1)} %get-tuple-element.98), channel_id=1, source_target_pairs={{0,2},{1,3},{2,0},{3,1},{4,6},{5,7},{6,4},{7,5},{8,10},{9,11},{10,... | collective-permute-start | bytes 442376 | tf_op jit(solution)/shard_map/ppermute | solution.py:561
  283.6 11.3 %collective-permute-start.20 = (bf16[96,768]{1,0:T(8,128)(2,1)S(1)}, bf16[96,768]{1,0:T(8,128)(2,1)S(1)}, u32[]{:S(2)}, u32[]{:S(2)}) collective-permute-start(bf16[96,768]{1,0:T(8,128)(2,1)S(1)} %get-tuple-element.98), channel_id=1, source_target_pairs={{0,3},{1,0},{2,1},{3,2},{4,7},{5,4},{6,5},{7,6},{8,11},{9,8},{10,9... | collective-permute-start | bytes 442376 | tf_op jit(solution)/shard_map/ppermute | solution.py:561
  295.1 6.2 %collective-permute-start.21 = (bf16[96,1344]{1,0:T(8,128)(2,1)S(1)}, bf16[96,1344]{1,0:T(8,128)(2,1)S(1)}, u32[]{:S(2)}, u32[]{:S(2)}) collective-permute-start(bf16[96,1344]{1,0:T(8,128)(2,1)S(1)} %pad_maximum_fusion.2), channel_id=1, source_target_pairs={{0,16},{4,20},{8,24},{12,28},{16,0},{20,4},{24,8},{28,12},{1,17},{... | collective-permute-start | bytes 774152 | tf_op jit(solution)/shard_map/ppermute | solution.py:590
  301.4 18.0 %collective-permute-start.22 = (bf16[192,1344]{1,0:T(8,128)(2,1)S(1)}, bf16[192,1344]{1,0:T(8,128)(2,1)S(1)}, u32[]{:S(2)}, u32[]{:S(2)}) collective-permute-start(bf16[192,1344]{1,0:T(8,128)(2,1)S(1)} %maximum_select_fusion.2), channel_id=1, source_target_pairs={{0,8},{4,12},{8,0},{12,4},{16,24},{20,28},{24,16},{28,20},{1,9},{5... | collective-permute-start | bytes 1548296 | tf_op jit(solution)/shard_map/ppermute | solution.py:590
  306.8 35.6 %collective-permute-start.10 = (bf16[256,768]{1,0:T(8,128)(2,1)}, bf16[256,768]{1,0:T(8,128)(2,1)}, u32[]{:S(2)}, u32[]{:S(2)}) collective-permute-start(bf16[256,768]{1,0:T(8,128)(2,1)} %get-tuple-element.88), channel_id=1, source_target_pairs={{0,2},{1,3},{2,0},{3,1},{4,6},{5,7},{6,4},{7,5},{8,10},{9,11},{10,... | collective-permute-start | bytes 1179656 | tf_op jit(solution)/shard_map/ppermute | solution.py:561
  316.1 26.3 %collective-permute-start.11 = (bf16[256,768]{1,0:T(8,128)(2,1)}, bf16[256,768]{1,0:T(8,128)(2,1)}, u32[]{:S(2)}, u32[]{:S(2)}) collective-permute-start(bf16[256,768]{1,0:T(8,128)(2,1)} %get-tuple-element.87), channel_id=1, source_target_pairs={{0,3},{1,0},{2,1},{3,2},{4,7},{5,4},{6,5},{7,6},{8,11},{9,8},{10,9... | collective-permute-start | bytes 1179656 | tf_op jit(solution)/shard_map/ppermute | solution.py:561
  316.1 45.3 %collective-permute-start.9 = (bf16[256,768]{1,0:T(8,128)(2,1)}, bf16[256,768]{1,0:T(8,128)(2,1)}, u32[]{:S(2)}, u32[]{:S(2)}) collective-permute-start(bf16[256,768]{1,0:T(8,128)(2,1)} %get-tuple-element.86), channel_id=1, source_target_pairs={{0,1},{1,2},{2,3},{3,0},{4,5},{5,6},{6,7},{7,4},{8,9},{9,10},{10,1... | collective-permute-start | bytes 1179656 | tf_op jit(solution)/shard_map/ppermute | solution.py:561
  321.2 100.3 %collective-permute-start.23 = (bf16[384,1344]{0,1:T(8,128)(2,1)}, bf16[384,1344]{0,1:T(8,128)(2,1)}, u32[]{:S(2)}, u32[]{:S(2)}) collective-permute-start(bf16[384,1344]{0,1:T(8,128)(2,1)} %copy.54), channel_id=1, source_target_pairs={{0,4},{4,0},{8,12},{12,8},{16,20},{20,16},{24,28},{28,24},{1,5},{5... | collective-permute-start | bytes 3096584 | tf_op jit(solution)/shard_map/ppermute | solution.py:590
  323.2 40.0 %collective-permute-start.3 = (bf16[256,768]{1,0:T(8,128)(2,1)S(1)}, bf16[256,768]{1,0:T(8,128)(2,1)S(1)}, u32[]{:S(2)}, u32[]{:S(2)}) collective-permute-start(bf16[256,768]{1,0:T(8,128)(2,1)S(1)} %copy-done.3), channel_id=1, source_target_pairs={{0,1},{1,2},{2,3},{3,0},{4,5},{5,6},{6,7},{7,4},{8,9},{9,10},{10,1... | collective-permute-start | bytes 1179656 | tf_op jit(solution)/shard_map/ppermute | solution.py:561
  342.4 50.5 %collective-permute-start.4 = (bf16[256,768]{1,0:T(8,128)(2,1)S(1)}, bf16[256,768]{1,0:T(8,128)(2,1)S(1)}, u32[]{:S(2)}, u32[]{:S(2)}) collective-permute-start(bf16[256,768]{1,0:T(8,128)(2,1)S(1)} %copy-done.3), channel_id=1, source_target_pairs={{0,2},{1,3},{2,0},{3,1},{4,6},{5,7},{6,4},{7,5},{8,10},{9,11},{10,... | collective-permute-start | bytes 1179656 | tf_op jit(solution)/shard_map/ppermute | solution.py:561
  342.4 51.2 %collective-permute-start.5 = (bf16[256,768]{1,0:T(8,128)(2,1)S(1)}, bf16[256,768]{1,0:T(8,128)(2,1)}, u32[]{:S(2)}, u32[]{:S(2)}) collective-permute-start(bf16[256,768]{1,0:T(8,128)(2,1)S(1)} %copy-done.3), channel_id=1, source_target_pairs={{0,3},{1,0},{2,1},{3,2},{4,7},{5,4},{6,5},{7,6},{8,11},{9,8},{10,9... | collective-permute-start | bytes 1179656 | tf_op jit(solution)/shard_map/ppermute | solution.py:561
  363.1 33.2 %copy-start.22 = (bf16[256,768]{1,0:T(8,128)(2,1)}, bf16[256,768]{1,0:T(8,128)(2,1)S(1)}, u32[]{:S(2)}) copy-start(bf16[256,768]{1,0:T(8,128)(2,1)S(1)} %fusion.7.refs_0_) | copy-start | bytes 1179652
  363.1 33.2 %collective-permute-start.12 = (bf16[256,768]{1,0:T(8,128)(2,1)S(1)}, bf16[256,768]{1,0:T(8,128)(2,1)S(1)}, u32[]{:S(2)}, u32[]{:S(2)}) collective-permute-start(bf16[256,768]{1,0:T(8,128)(2,1)S(1)} %fusion.7.refs_0_), channel_id=1, source_target_pairs={{0,1},{1,2},{2,3},{3,0},{4,5},{5,6},{6,7},{7,4},{8,9},{9,10},{10,1... | collective-permute-start | bytes 1179656 | tf_op jit(solution)/shard_map/ppermute | solution.py:561
  363.1 30.5 %copy-start.23 = (bf16[256,768]{1,0:T(8,128)(2,1)}, bf16[256,768]{1,0:T(8,128)(2,1)S(1)}, u32[]{:S(2)}) copy-start(bf16[256,768]{1,0:T(8,128)(2,1)S(1)} %collective-permute-done.3.refs_1_) | copy-start | bytes 1179652
  363.2 55.0 %collective-permute-start.13 = (bf16[256,768]{1,0:T(8,128)(2,1)S(1)}, bf16[256,768]{1,0:T(8,128)(2,1)S(1)}, u32[]{:S(2)}, u32[]{:S(2)}) collective-permute-start(bf16[256,768]{1,0:T(8,128)(2,1)S(1)} %fusion.7.refs_0_), channel_id=1, source_target_pairs={{0,2},{1,3},{2,0},{3,1},{4,6},{5,7},{6,4},{7,5},{8,10},{9,11},{10,... | collective-permute-start | bytes 1179656 | tf_op jit(solution)/shard_map/ppermute | solution.py:561
  393.6 24.5 %collective-permute-start.14 = (bf16[256,768]{1,0:T(8,128)(2,1)S(1)}, bf16[256,768]{1,0:T(8,128)(2,1)}, u32[]{:S(2)}, u32[]{:S(2)}) collective-permute-start(bf16[256,768]{1,0:T(8,128)(2,1)S(1)} %fusion.7.refs_0_), channel_id=1, source_target_pairs={{0,3},{1,0},{2,1},{3,2},{4,7},{5,4},{6,5},{7,6},{8,11},{9,8},{10,9... | collective-permute-start | bytes 1179656 | tf_op jit(solution)/shard_map/ppermute | solution.py:561
  (33 other events, 130.4 us)
Sparse Core Ops, SparseCore 0:
  11.4 97.0 all-gather.4
  130.6 83.6 reduce-scatter.2
  216.5 31.0 reduce-scatter.4
  277.7 35.0 all-gather.6
